TPU v7x, 256 devices: a whole 4x4x8 slice. The times are simulated.
256 devices in a mesh: gz: 8 (over z_lo, x), gy: 8 (over z_hi, core), gx: 4 (over y).
Axes of the slice: x: 4, y: 4, z: 8 (z_hi: 4, z_lo: 2; z = z_hi * 2 + z_lo), core: 2. Of those that a mesh axis runs over, the one named last changes fastest.
Arguments:
- volume: bfloat16 [16, 64, 128, 512], P(None, 'gz', 'gy', 'gx'), may hold values from -6 to 6
- surface_conv: bfloat16 [16, 16, 3, 3, 3], replicated, may hold values from -0.4375 to 0.4375
- surface_bias: float32 [16], replicated, may hold values from -3 to 3
- second_conv: bfloat16 [32, 16, 3, 3, 3], replicated, may hold values from -0.4375 to 0.4375
- second_bias: float32 [32], replicated, may hold values from -3 to 3
- middle_conv: bfloat16 [64, 32, 3, 3, 3], replicated, may hold values from -0.3125 to 0.3125
- middle_bias: float32 [64], replicated, may hold values from -3 to 3
- bottom_conv: bfloat16 [128, 64, 3, 3, 3], replicated, may hold values from -0.21875 to 0.21875
- bottom_bias: float32 [128], replicated, may hold values from -3 to 3
- middle_lift: bfloat16 [64, 128], replicated, may hold values from -0.75 to 0.75
- middle_return: bfloat16 [64, 128, 3, 3, 3], replicated, may hold values from -0.15625 to 0.15625
- middle_offset: float32 [64], replicated, may hold values from -3 to 3
- second_lift: bfloat16 [32, 64], replicated, may hold values from -1 to 1
- second_return: bfloat16 [32, 64, 3, 3, 3], replicated, may hold values from -0.21875 to 0.21875
- second_offset: float32 [32], replicated, may hold values from -3 to 3
- surface_lift: bfloat16 [16, 32], replicated, may hold values from -1.5 to 1.5
- surface_return: bfloat16 [16, 32, 3, 3, 3], replicated, may hold values from -0.3125 to 0.3125
- surface_offset: float32 [16], replicated, may hold values from -3 to 3
Outputs:
- decoded: bfloat16 [16, 64, 128, 512], P(None, 'gz', 'gy', 'gx')
All inputs are finite; a program needn't handle non-finite values.
Results may differ from a plain program's by a relative error of at most 0.024.
Values may be sent and summed in bfloat16 or wider, within the bound.
A program may use at most 128 MiB of HBM per device.

v0:
```python
import jax
import jax.numpy as jnp
from jax import lax
from jax.sharding import PartitionSpec as P


def extended(cells, sides, width):
    for axis, dim in sides:
        count = lax.axis_size(axis)
        ends = count - 1
        head = lax.slice_in_dim(cells, 0, width, axis=dim)
        tail = lax.slice_in_dim(cells, cells.shape[dim] - width, cells.shape[dim], axis=dim)
        cells = jnp.concatenate(
            [
                lax.ppermute(tail, axis, [(i, (i + 1) % count) for i in range(ends)]),
                cells,
                lax.ppermute(head, axis, [((i + 1) % count, i) for i in range(ends)]),
            ],
            axis=dim,
        )
    return cells


def convolve(padded, kernel, offset):
    outputs = kernel.shape[0]
    inputs = kernel.shape[1]
    depth = padded.shape[1] - 2
    height = padded.shape[2] - 2
    width = padded.shape[3] - 2
    stacked = jnp.concatenate([padded[:, :, :, c : c + width] for c in range(3)], axis=0)
    total = jnp.zeros((outputs, depth, height, width), jnp.float32)
    for a in range(3):
        for b in range(3):
            taps = jnp.transpose(kernel[:, :, a, b, :], (0, 2, 1)).reshape(outputs, 3 * inputs)
            window = stacked[:, a : a + depth, b : b + height, :]
            total = total + jnp.einsum(
                "ok,kdhw->odhw", taps, window, preferred_element_type=jnp.float32
            )
    total = total + offset[:, None, None, None]
    return jnp.maximum(total, 0.1 * total).astype(jnp.bfloat16)


def pooled(values):
    chans, depth, height, width = values.shape
    return values.reshape(chans, depth // 2, 2, height // 2, 2, width // 2, 2).max(axis=(2, 4, 6))


def upsampled(values):
    chans, depth, height, width = values.shape
    grown = jnp.broadcast_to(
        values[:, :, None, :, None, :, None], (chans, depth, 2, height, 2, width, 2)
    )
    return grown.reshape(chans, 2 * depth, 2 * height, 2 * width)


def lifted(matrix, values):
    return jnp.einsum("oi,idhw->odhw", matrix, values, preferred_element_type=jnp.float32).astype(
        jnp.bfloat16
    )


def full_rim(values):
    return extended(values, (("gz", 1), ("gy", 2), ("gx", 3)), 1)


def coarse_rim(values):
    return extended(values, (("gz", 1), ("gy", 2), ("gx", 3)), 1)


def per_device(
    volume,
    surface_conv,
    surface_bias,
    second_conv,
    second_bias,
    middle_conv,
    middle_bias,
    bottom_conv,
    bottom_bias,
    middle_lift,
    middle_return,
    middle_offset,
    second_lift,
    second_return,
    second_offset,
    surface_lift,
    surface_return,
    surface_offset,
):
    skip_zero = convolve(full_rim(volume), surface_conv, surface_bias)
    skip_one = convolve(full_rim(pooled(skip_zero)), second_conv, second_bias)
    skip_two = convolve(coarse_rim(pooled(skip_one)), middle_conv, middle_bias)
    bottom = convolve(coarse_rim(pooled(skip_two)), bottom_conv, bottom_bias)
    lift_two = lifted(middle_lift, bottom)
    joined_two = jnp.concatenate([skip_two, upsampled(lift_two)], axis=0)
    upper_two = convolve(coarse_rim(joined_two), middle_return, middle_offset)
    lift_one = lifted(second_lift, upper_two)
    joined_one = jnp.concatenate([skip_one, upsampled(lift_one)], axis=0)
    upper_one = convolve(full_rim(joined_one), second_return, second_offset)
    lift_zero = lifted(surface_lift, upper_one)
    padded = full_rim(jnp.concatenate([skip_zero, upsampled(lift_zero)], axis=0))
    return convolve(padded, surface_return, surface_offset)


def solution(mesh):
    placed = (
        P(None, "gz", "gy", "gx"),
        P(),
        P(),
        P(),
        P(),
        P(),
        P(),
        P(),
        P(),
        P(),
        P(),
        P(),
        P(),
        P(),
        P(),
        P(),
        P(),
        P(),
    )
    return jax.shard_map(
        per_device, mesh=mesh, in_specs=placed, out_specs=P(None, "gz", "gy", "gx"), check_vma=False
    )
```

profile of v0, /device:TPU:79, one launch (start us, length us, event | category | flops | bytes accessed | tf_op | source)
XLA Modules:
  0.0 328.2 jit_solution(4648665406674481440)
XLA Ops:
  0.9 3.5 %collective-permute-start = (bf16[16,1,16,128]{3,0,2,1:T(8,128)(2,1)S(1)}, bf16[16,1,16,128]{3,0,2,1:T(8,128)(2,1)S(1)}, u32[]{:S(2)}, u32[]{:S(2)}) collective-permute-start(bf16[16,1,16,128]{3,0,2,1:T(8,128)(2,1)S(1)} %copy.330), channel_id=1, source_target_pairs={{0,32},{32,64},{64,96},{96,128},{128,160},{160,192},{192,224},{1,3... | collective-permute-start | bytes 196616 | tf_op jit(solution)/shard_map/ppermute | solution.py:15
  7.8 3.7 %collective-permute-done.1 = bf16[16,1,16,128]{3,0,2,1:T(8,128)(2,1)S(1)} collective-permute-done((bf16[16,1,16,128]{3,0,2,1:T(8,128)(2,1)S(1)}, bf16[16,1,16,128]{3,0,2,1:T(8,128)(2,1)S(1)}, u32[]{:S(2)}, u32[]{:S(2)}) %collective-permute-start.1) | collective-permute-done | bytes 65568 | tf_op jit(solution)/shard_map/ppermute | solution.py:17
  11.6 7.2 %collective-permute-start.2 = (bf16[16,10,1,128]{3,0,2,1:T(8,128)(2,1)S(1)}, bf16[16,10,1,128]{3,0,2,1:T(8,128)(2,1)S(1)}, u32[]{:S(2)}, u32[]{:S(2)}) collective-permute-start(bf16[16,10,1,128]{3,0,2,1:T(8,128)(2,1)S(1)} %get-tuple-element.17), channel_id=1, source_target_pairs={{0,4},{4,8},{8,12},{12,16},{16,20},{20,24},{24,28},{1,5},{5,9},{9,... | collective-permute-start | bytes 122888 | tf_op jit(solution)/shard_map/ppermute | solution.py:15
  20.9 5.5 %collective-permute-done.3 = bf16[16,10,1,128]{3,0,2,1:T(8,128)(2,1)S(1)} collective-permute-done((bf16[16,10,1,128]{3,0,2,1:T(8,128)(2,1)S(1)}, bf16[16,10,1,128]{3,0,2,1:T(8,128)(2,1)S(1)}, u32[]{:S(2)}, u32[]{:S(2)}) %collective-permute-start.3) | collective-permute-done | bytes 40992 | tf_op jit(solution)/shard_map/ppermute | solution.py:17
  38.0 3.6 %fusion.22 = bf16[48,10,18,128]{3,0,2,1:T(8,128)(2,1)S(1)} fusion(bf16[16,10,18,1]{3,0,2,1:T(8,128)(2,1)S(1)} %copy.165, bf16[16,10,1,128]{3,0,2,1:T(8,128)(2,1)S(1)} %collective-permute-done.3, bf16[16,10,16,128]{3,0,2,1:T(8,128)(2,1)S(1)} %constant_dynamic-update-slice_fusion, bf16[16,10,1,128]{3,0,2,1:T(8,128)(2,1)S(1)} %collective-permute-done.2, ...), kind=kLoop, calls=%fused_computation.47 | loop fusion | flops 24330240 | bytes 2960640 | tf_op jit(solution)/shard_map/concatenate | solution.py:30
  48.0 8.3 %reduce_max.36 = bf16[16,4,8,64]{0,3,2,1:T(8,128)(2,1)S(1)} reduce(bf16[16,4,2,8,2,64,2]{0,6,5,4,3,2,1:T(2,128)(2,1)} %bitcast.600, bf16[]{:T(256)} %constant.3.clone.1), dimensions={2,4,6}, to_apply=%region_0.0 | reduce | flops 229376 | bytes 589826 | tf_op jit(solution)/shard_map/reduce_max | solution.py:45
  61.9 3.4 %collective-permute-done.7 = bf16[16,1,8,64]{3,0,2,1:T(8,128)(2,1)S(1)} collective-permute-done((bf16[16,1,8,64]{3,0,2,1:T(8,128)(2,1)S(1)}, bf16[16,1,8,64]{3,0,2,1:T(8,128)(2,1)S(1)}, u32[]{:S(2)}, u32[]{:S(2)}) %collective-permute-start.7) | collective-permute-done | bytes 16416 | tf_op jit(solution)/shard_map/ppermute | solution.py:17
  65.3 4.5 %collective-permute-start.8 = (bf16[16,6,1,64]{3,0,2,1:T(8,128)(2,1)S(1)}, bf16[16,6,1,64]{3,0,2,1:T(8,128)(2,1)S(1)}, u32[]{:S(2)}, u32[]{:S(2)}) collective-permute-start(bf16[16,6,1,64]{3,0,2,1:T(8,128)(2,1)S(1)} %get-tuple-element.67), channel_id=1, source_target_pairs={{0,4},{4,8},{8,12},{12,16},{16,20},{20,24},{24,28},{1,5},{5,9},{9,... | collective-permute-start | bytes 36872 | tf_op jit(solution)/shard_map/ppermute | solution.py:15
  71.7 5.3 %collective-permute-done.9 = bf16[16,6,1,64]{3,0,2,1:T(8,128)(2,1)S(1)} collective-permute-done((bf16[16,6,1,64]{3,0,2,1:T(8,128)(2,1)S(1)}, bf16[16,6,1,64]{3,0,2,1:T(8,128)(2,1)S(1)}, u32[]{:S(2)}, u32[]{:S(2)}) %collective-permute-start.9) | collective-permute-done | bytes 12320 | tf_op jit(solution)/shard_map/ppermute | solution.py:17
  98.6 3.4 %collective-permute-done.13 = bf16[32,1,4,32]{0,3,2,1:T(8,128)(2,1)S(1)} collective-permute-done((bf16[32,1,4,32]{0,3,2,1:T(8,128)(2,1)S(1)}, bf16[32,1,4,32]{0,3,2,1:T(8,128)(2,1)S(1)}, u32[]{:S(2)}, u32[]{:S(2)}) %collective-permute-start.13) | collective-permute-done | bytes 8224 | tf_op jit(solution)/shard_map/ppermute | solution.py:17
  102.0 5.0 %collective-permute-start.14 = (bf16[32,4,1,32]{0,3,2,1:T(8,128)(2,1)S(1)}, bf16[32,4,1,32]{0,3,2,1:T(8,128)(2,1)S(1)}, u32[]{:S(2)}, u32[]{:S(2)}) collective-permute-start(bf16[32,4,1,32]{0,3,2,1:T(8,128)(2,1)S(1)} %get-tuple-element.71), channel_id=1, source_target_pairs={{0,4},{4,8},{8,12},{12,16},{16,20},{20,24},{24,28},{1,5},{5,9},{9,... | collective-permute-start | bytes 24584 | tf_op jit(solution)/shard_map/ppermute | solution.py:15
  108.9 5.4 %collective-permute-done.15 = bf16[32,4,1,32]{0,3,2,1:T(8,128)(2,1)S(1)} collective-permute-done((bf16[32,4,1,32]{0,3,2,1:T(8,128)(2,1)S(1)}, bf16[32,4,1,32]{0,3,2,1:T(8,128)(2,1)S(1)}, u32[]{:S(2)}, u32[]{:S(2)}) %collective-permute-start.15) | collective-permute-done | bytes 8224 | tf_op jit(solution)/shard_map/ppermute | solution.py:17
  125.7 5.5 %collective-permute-start.18 = (bf16[64,1,2,16]{0,3,2,1:T(8,128)(2,1)S(1)}, bf16[64,1,2,16]{0,3,2,1:T(8,128)(2,1)S(1)}, u32[]{:S(2)}, u32[]{:S(2)}) collective-permute-start(bf16[64,1,2,16]{0,3,2,1:T(8,128)(2,1)S(1)} %bitcast.615), channel_id=1, source_target_pairs={{0,32},{32,64},{64,96},{96,128},{128,160},{160,192},{192,224},{1,3... | collective-permute-start | bytes 12296 | tf_op jit(solution)/shard_map/ppermute | solution.py:15
  132.0 4.5 %collective-permute-start.20 = (bf16[64,3,1,16]{0,3,2,1:T(8,128)(2,1)S(1)}, bf16[64,3,1,16]{0,3,2,1:T(8,128)(2,1)S(1)}, u32[]{:S(2)}, u32[]{:S(2)}) collective-permute-start(bf16[64,3,1,16]{0,3,2,1:T(8,128)(2,1)S(1)} %get-tuple-element.106), channel_id=1, source_target_pairs={{0,4},{4,8},{8,12},{12,16},{16,20},{20,24},{24,28},{1,5},{5,9},{9,... | collective-permute-start | bytes 18440 | tf_op jit(solution)/shard_map/ppermute | solution.py:15
  138.4 5.2 %collective-permute-done.21 = bf16[64,3,1,16]{0,3,2,1:T(8,128)(2,1)S(1)} collective-permute-done((bf16[64,3,1,16]{0,3,2,1:T(8,128)(2,1)S(1)}, bf16[64,3,1,16]{0,3,2,1:T(8,128)(2,1)S(1)}, u32[]{:S(2)}, u32[]{:S(2)}) %collective-permute-start.21) | collective-permute-done | bytes 6176 | tf_op jit(solution)/shard_map/ppermute | solution.py:17
  151.6 6.1 %collective-permute-start.24 = (bf16[128,1,4,32]{0,3,2,1:T(8,128)(2,1)S(1)}, bf16[128,1,4,32]{0,3,2,1:T(8,128)(2,1)S(1)}, u32[]{:S(2)}, u32[]{:S(2)}) collective-permute-start(bf16[128,1,4,32]{0,3,2,1:T(8,128)(2,1)S(1)} %get-tuple-element.69), channel_id=1, source_target_pairs={{0,32},{32,64},{64,96},{96,128},{128,160},{160,192},{192,224},{1,3... | collective-permute-start | bytes 98312 | tf_op jit(solution)/shard_map/ppermute | solution.py:15
  159.6 4.8 %collective-permute-done.25 = bf16[128,1,4,32]{0,3,2,1:T(8,128)(2,1)S(1)} collective-permute-done((bf16[128,1,4,32]{0,3,2,1:T(8,128)(2,1)S(1)}, bf16[128,1,4,32]{0,3,2,1:T(8,128)(2,1)S(1)}, u32[]{:S(2)}, u32[]{:S(2)}) %collective-permute-start.25) | collective-permute-done | bytes 32800 | tf_op jit(solution)/shard_map/ppermute | solution.py:17
  164.5 4.5 %collective-permute-start.26 = (bf16[128,4,1,32]{0,3,2,1:T(8,128)(2,1)S(1)}, bf16[128,4,1,32]{0,3,2,1:T(8,128)(2,1)S(1)}, u32[]{:S(2)}, u32[]{:S(2)}) collective-permute-start(bf16[128,4,1,32]{0,3,2,1:T(8,128)(2,1)S(1)} %get-tuple-element.63), channel_id=1, source_target_pairs={{0,4},{4,8},{8,12},{12,16},{16,20},{20,24},{24,28},{1,5},{5,9},{9,... | collective-permute-start | bytes 98312 | tf_op jit(solution)/shard_map/ppermute | solution.py:15
  171.0 5.4 %collective-permute-done.27 = bf16[128,4,1,32]{0,3,2,1:T(8,128)(2,1)S(1)} collective-permute-done((bf16[128,4,1,32]{0,3,2,1:T(8,128)(2,1)S(1)}, bf16[128,4,1,32]{0,3,2,1:T(8,128)(2,1)S(1)}, u32[]{:S(2)}, u32[]{:S(2)}) %collective-permute-start.27) | collective-permute-done | bytes 32800 | tf_op jit(solution)/shard_map/ppermute | solution.py:17
  191.6 4.0 %collective-permute-done.31 = bf16[64,1,8,64]{3,0,2,1:T(8,128)(2,1)S(1)} collective-permute-done((bf16[64,1,8,64]{3,0,2,1:T(8,128)(2,1)S(1)}, bf16[64,1,8,64]{3,0,2,1:T(8,128)(2,1)S(1)}, u32[]{:S(2)}, u32[]{:S(2)}) %collective-permute-start.31) | collective-permute-done | bytes 65568 | tf_op jit(solution)/shard_map/ppermute | solution.py:17
  195.7 5.3 %collective-permute-start.32 = (bf16[64,6,1,64]{3,0,2,1:T(8,128)(2,1)S(1)}, bf16[64,6,1,64]{3,0,2,1:T(8,128)(2,1)S(1)}, u32[]{:S(2)}, u32[]{:S(2)}) collective-permute-start(bf16[64,6,1,64]{3,0,2,1:T(8,128)(2,1)S(1)} %get-tuple-element.13), channel_id=1, source_target_pairs={{0,4},{4,8},{8,12},{12,16},{16,20},{20,24},{24,28},{1,5},{5,9},{9,... | collective-permute-start | bytes 147464 | tf_op jit(solution)/shard_map/ppermute | solution.py:15
  202.9 6.1 %collective-permute-done.33 = bf16[64,6,1,64]{3,0,2,1:T(8,128)(2,1)S(1)} collective-permute-done((bf16[64,6,1,64]{3,0,2,1:T(8,128)(2,1)S(1)}, bf16[64,6,1,64]{3,0,2,1:T(8,128)(2,1)S(1)}, u32[]{:S(2)}, u32[]{:S(2)}) %collective-permute-start.33) | collective-permute-done | bytes 49184 | tf_op jit(solution)/shard_map/ppermute | solution.py:17
  211.6 3.6 %collective-permute-start.35 = (bf16[64,6,10,1]{0,1,3,2:T(8,128)(2,1)S(1)}, bf16[64,6,10,1]{0,1,3,2:T(8,128)(2,1)S(1)}, u32[]{:S(2)}, u32[]{:S(2)}) collective-permute-start(bf16[64,6,10,1]{0,1,3,2:T(8,128)(2,1)S(1)} %copy.210), channel_id=1, source_target_pairs={{1,0},{2,1},{3,2},{5,4},{6,5},{7,6},{9,8},{10,9},{11,10},{13,12},{... | collective-permute-start | bytes 23048 | tf_op jit(solution)/shard_map/ppermute | solution.py:17
  223.4 13.3 %fusion.20 = bf16[192,6,10,64]{3,0,2,1:T(8,128)(2,1)S(1)} fusion(bf16[64,6,10,1]{3,0,2,1:T(8,128)(2,1)} %copy.211, bf16[64,6,1,64]{3,0,2,1:T(8,128)(2,1)} %copy-done.9, bf16[64,6,1,64]{3,0,2,1:T(8,128)(2,1)} %copy-done.8, bf16[64,1,8,64]{3,0,2,1:T(8,128)(2,1)} %copy-done.5, bf16[64,1,8,64]{3,0,2,1:T(8,128)(2,1)} %copy-done.4, ...), kind=kLoop, calls=%fused_computation.33 | loop fusion | flops 29491200 | bytes 1981440 | tf_op jit(solution)/shard_map/concatenate | solution.py:30
  246.3 3.5 %fusion.175 = bf16[16,4,8,64]{3,0,2,1:T(8,128)(2,1)} fusion(f32[4,8,64,32]{2,3,1,0:T(8,128)} %fusion.24, f32[4,8,64,32]{2,3,1,0:T(8,128)} %fusion.26, f32[4,8,64,32]{2,3,1,0:T(8,128)} %fusion.28, f32[4,8,64,32]{2,3,1,0:T(8,128)} %fusion.30, f32[4,8,64,32]{2,3,1,0:T(8,128)} %fusion.32, f32[4,8,64,32]{2,3,1,0:T(8,128)} %fusion.34, ...), kind=kOutput, calls=%fused_computation.143 | convolution fusion | flops 28082176 | bytes 3756544 | tf_op jit(solution)/shard_map/oi,idhw->odhw/dot_general | solution.py:57
  251.0 6.2 %broadcast_in_dim.14 = bf16[16,4,2,8,2,64,2]{0,6,5,4,3,2,1:T(2,128)(2,1)} broadcast(bf16[16,4,8,64]{0,3,2,1:T(8,128)(2,1)S(1)} %copy.230), dimensions={0,1,3,5} | broadcast | bytes 589824 | tf_op jit(solution)/shard_map/broadcast_in_dim | solution.py:50
  257.2 3.5 %copy.231 = bf16[16,8,16,128]{3,0,2,1:T(8,128)(2,1)S(1)} copy(bf16[16,8,16,128]{0,3,2,1:T(8,128)(2,1)} %bitcast.599) | data formatting | bytes 1048576 | tf_op jit(solution)/shard_map/reshape | solution.py:53
  266.7 3.7 %collective-permute-done.37 = bf16[32,1,16,128]{3,0,2,1:T(8,128)(2,1)S(1)} collective-permute-done((bf16[32,1,16,128]{3,0,2,1:T(8,128)(2,1)S(1)}, bf16[32,1,16,128]{3,0,2,1:T(8,128)(2,1)S(1)}, u32[]{:S(2)}, u32[]{:S(2)}) %collective-permute-start.37) | collective-permute-done | bytes 131104 | tf_op jit(solution)/shard_map/ppermute | solution.py:17
  270.5 4.2 %collective-permute-start.38 = (bf16[32,10,1,128]{3,0,2,1:T(8,128)(2,1)S(1)}, bf16[32,10,1,128]{3,0,2,1:T(8,128)(2,1)S(1)}, u32[]{:S(2)}, u32[]{:S(2)}) collective-permute-start(bf16[32,10,1,128]{3,0,2,1:T(8,128)(2,1)S(1)} %get-tuple-element.7), channel_id=1, source_target_pairs={{0,4},{4,8},{8,12},{12,16},{16,20},{20,24},{24,28},{1,5},{5,9},{9,... | collective-permute-start | bytes 245768 | tf_op jit(solution)/shard_map/ppermute | solution.py:15
  276.6 5.9 %collective-permute-done.39 = bf16[32,10,1,128]{3,0,2,1:T(8,128)(2,1)S(1)} collective-permute-done((bf16[32,10,1,128]{3,0,2,1:T(8,128)(2,1)S(1)}, bf16[32,10,1,128]{3,0,2,1:T(8,128)(2,1)S(1)}, u32[]{:S(2)}, u32[]{:S(2)}) %collective-permute-start.39) | collective-permute-done | bytes 81952 | tf_op jit(solution)/shard_map/ppermute | solution.py:17
  289.0 3.4 %collective-permute-start.41 = (bf16[32,10,18,1]{0,2,3,1:T(8,128)(2,1)S(1)}, bf16[32,10,18,1]{0,2,3,1:T(8,128)(2,1)S(1)}, u32[]{:S(2)}, u32[]{:S(2)}) collective-permute-start(bf16[32,10,18,1]{0,2,3,1:T(8,128)(2,1)S(1)} %copy.234), channel_id=1, source_target_pairs={{1,0},{2,1},{3,2},{5,4},{6,5},{7,6},{9,8},{10,9},{11,10},{13,12},{... | collective-permute-start | bytes 34568 | tf_op jit(solution)/shard_map/ppermute | solution.py:17
  300.8 21.1 %fusion = bf16[96,10,18,128]{3,0,2,1:T(8,128)(2,1)S(1)} fusion(bf16[32,10,18,1]{3,0,2,1:T(8,128)(2,1)} %copy.235, bf16[32,10,1,128]{3,0,2,1:T(8,128)(2,1)S(1)} %collective-permute-done.39, bf16[32,10,1,128]{3,0,2,1:T(8,128)(2,1)S(1)} %collective-permute-done.38, bf16[32,1,16,128]{3,0,2,1:T(8,128)(2,1)S(1)} %collective-permute-done.37, ...), kind=kLoop, calls=%fused_computation.1 | loop fusion | flops 88473600 | bytes 5921280 | tf_op jit(solution)/shard_map/concatenate | solution.py:30
  (313 shorter events, 147.9 us)
Async XLA Ops:
  0.9 5.4 %collective-permute-start = (bf16[16,1,16,128]{3,0,2,1:T(8,128)(2,1)S(1)}, bf16[16,1,16,128]{3,0,2,1:T(8,128)(2,1)S(1)}, u32[]{:S(2)}, u32[]{:S(2)}) collective-permute-start(bf16[16,1,16,128]{3,0,2,1:T(8,128)(2,1)S(1)} %copy.330), channel_id=1, source_target_pairs={{0,32},{32,64},{64,96},{96,128},{128,160},{160,192},{192,224},{1,3... | collective-permute-start | bytes 196616 | tf_op jit(solution)/shard_map/ppermute | solution.py:15
  4.4 7.1 %collective-permute-start.1 = (bf16[16,1,16,128]{3,0,2,1:T(8,128)(2,1)S(1)}, bf16[16,1,16,128]{3,0,2,1:T(8,128)(2,1)S(1)}, u32[]{:S(2)}, u32[]{:S(2)}) collective-permute-start(bf16[16,1,16,128]{3,0,2,1:T(8,128)(2,1)S(1)} %copy.331), channel_id=1, source_target_pairs={{32,0},{64,32},{96,64},{128,96},{160,128},{192,160},{224,192},{33,... | collective-permute-start | bytes 196616 | tf_op jit(solution)/shard_map/ppermute | solution.py:17
  11.6 9.3 %collective-permute-start.2 = (bf16[16,10,1,128]{3,0,2,1:T(8,128)(2,1)S(1)}, bf16[16,10,1,128]{3,0,2,1:T(8,128)(2,1)S(1)}, u32[]{:S(2)}, u32[]{:S(2)}) collective-permute-start(bf16[16,10,1,128]{3,0,2,1:T(8,128)(2,1)S(1)} %get-tuple-element.17), channel_id=1, source_target_pairs={{0,4},{4,8},{8,12},{12,16},{16,20},{20,24},{24,28},{1,5},{5,9},{9,... | collective-permute-start | bytes 122888 | tf_op jit(solution)/shard_map/ppermute | solution.py:15
  18.8 7.6 %collective-permute-start.3 = (bf16[16,10,1,128]{3,0,2,1:T(8,128)(2,1)S(1)}, bf16[16,10,1,128]{3,0,2,1:T(8,128)(2,1)S(1)}, u32[]{:S(2)}, u32[]{:S(2)}) collective-permute-start(bf16[16,10,1,128]{3,0,2,1:T(8,128)(2,1)S(1)} %get-tuple-element.18), channel_id=1, source_target_pairs={{4,0},{8,4},{12,8},{16,12},{20,16},{24,20},{28,24},{5,1},{9,5},{13... | collective-permute-start | bytes 122888 | tf_op jit(solution)/shard_map/ppermute | solution.py:17
  28.9 7.9 %collective-permute-start.5 = (bf16[16,10,18,1]{2,0,3,1:T(8,128)(2,1)S(1)}, bf16[16,10,18,1]{2,0,3,1:T(8,128)(2,1)S(1)}, u32[]{:S(2)}, u32[]{:S(2)}) collective-permute-start(bf16[16,10,18,1]{2,0,3,1:T(8,128)(2,1)S(1)} %copy.164), channel_id=1, source_target_pairs={{1,0},{2,1},{3,2},{5,4},{6,5},{7,6},{9,8},{10,9},{11,10},{13,12},{... | collective-permute-start | bytes 17288 | tf_op jit(solution)/shard_map/ppermute | solution.py:17
  58.5 6.8 %collective-permute-start.7 = (bf16[16,1,8,64]{3,0,2,1:T(8,128)(2,1)S(1)}, bf16[16,1,8,64]{3,0,2,1:T(8,128)(2,1)S(1)}, u32[]{:S(2)}, u32[]{:S(2)}) collective-permute-start(bf16[16,1,8,64]{3,0,2,1:T(8,128)(2,1)S(1)} %get-tuple-element.74), channel_id=1, source_target_pairs={{32,0},{64,32},{96,64},{128,96},{160,128},{192,160},{224,192},{33,... | collective-permute-start | bytes 49160 | tf_op jit(solution)/shard_map/ppermute | solution.py:17
  65.3 6.4 %collective-permute-start.8 = (bf16[16,6,1,64]{3,0,2,1:T(8,128)(2,1)S(1)}, bf16[16,6,1,64]{3,0,2,1:T(8,128)(2,1)S(1)}, u32[]{:S(2)}, u32[]{:S(2)}) collective-permute-start(bf16[16,6,1,64]{3,0,2,1:T(8,128)(2,1)S(1)} %get-tuple-element.67), channel_id=1, source_target_pairs={{0,4},{4,8},{8,12},{12,16},{16,20},{20,24},{24,28},{1,5},{5,9},{9,... | collective-permute-start | bytes 36872 | tf_op jit(solution)/shard_map/ppermute | solution.py:15
  69.8 7.3 %collective-permute-start.9 = (bf16[16,6,1,64]{3,0,2,1:T(8,128)(2,1)S(1)}, bf16[16,6,1,64]{3,0,2,1:T(8,128)(2,1)S(1)}, u32[]{:S(2)}, u32[]{:S(2)}) collective-permute-start(bf16[16,6,1,64]{3,0,2,1:T(8,128)(2,1)S(1)} %get-tuple-element.68), channel_id=1, source_target_pairs={{4,0},{8,4},{12,8},{16,12},{20,16},{24,20},{28,24},{5,1},{9,5},{13... | collective-permute-start | bytes 36872 | tf_op jit(solution)/shard_map/ppermute | solution.py:17
  77.3 7.0 %collective-permute-start.10 = (bf16[16,6,10,1]{3,0,2,1:T(8,128)(2,1)S(1)}, bf16[16,6,10,1]{3,0,2,1:T(8,128)(2,1)S(1)}, u32[]{:S(2)}, u32[]{:S(2)}) collective-permute-start(bf16[16,6,10,1]{3,0,2,1:T(8,128)(2,1)S(1)} %get-tuple-element.43), channel_id=1, source_target_pairs={{0,1},{1,2},{2,3},{4,5},{5,6},{6,7},{8,9},{9,10},{10,11},{12,13},{... | collective-permute-start | bytes 5768 | tf_op jit(solution)/shard_map/ppermute | solution.py:15
  80.5 6.9 %collective-permute-start.11 = (bf16[16,6,10,1]{3,0,2,1:T(8,128)(2,1)S(1)}, bf16[16,6,10,1]{3,0,2,1:T(8,128)(2,1)S(1)}, u32[]{:S(2)}, u32[]{:S(2)}) collective-permute-start(bf16[16,6,10,1]{3,0,2,1:T(8,128)(2,1)S(1)} %get-tuple-element.44), channel_id=1, source_target_pairs={{1,0},{2,1},{3,2},{5,4},{6,5},{7,6},{9,8},{10,9},{11,10},{13,12},{... | collective-permute-start | bytes 5768 | tf_op jit(solution)/shard_map/ppermute | solution.py:17
  95.2 6.8 %collective-permute-start.13 = (bf16[32,1,4,32]{0,3,2,1:T(8,128)(2,1)S(1)}, bf16[32,1,4,32]{0,3,2,1:T(8,128)(2,1)S(1)}, u32[]{:S(2)}, u32[]{:S(2)}) collective-permute-start(bf16[32,1,4,32]{0,3,2,1:T(8,128)(2,1)S(1)} %get-tuple-element.103), channel_id=1, source_target_pairs={{32,0},{64,32},{96,64},{128,96},{160,128},{192,160},{224,192},{33,... | collective-permute-start | bytes 24584 | tf_op jit(solution)/shard_map/ppermute | solution.py:17
  102.0 7.0 %collective-permute-start.14 = (bf16[32,4,1,32]{0,3,2,1:T(8,128)(2,1)S(1)}, bf16[32,4,1,32]{0,3,2,1:T(8,128)(2,1)S(1)}, u32[]{:S(2)}, u32[]{:S(2)}) collective-permute-start(bf16[32,4,1,32]{0,3,2,1:T(8,128)(2,1)S(1)} %get-tuple-element.71), channel_id=1, source_target_pairs={{0,4},{4,8},{8,12},{12,16},{16,20},{20,24},{24,28},{1,5},{5,9},{9,... | collective-permute-start | bytes 24584 | tf_op jit(solution)/shard_map/ppermute | solution.py:15
  107.0 7.3 %collective-permute-start.15 = (bf16[32,4,1,32]{0,3,2,1:T(8,128)(2,1)S(1)}, bf16[32,4,1,32]{0,3,2,1:T(8,128)(2,1)S(1)}, u32[]{:S(2)}, u32[]{:S(2)}) collective-permute-start(bf16[32,4,1,32]{0,3,2,1:T(8,128)(2,1)S(1)} %get-tuple-element.72), channel_id=1, source_target_pairs={{4,0},{8,4},{12,8},{16,12},{20,16},{24,20},{28,24},{5,1},{9,5},{13... | collective-permute-start | bytes 24584 | tf_op jit(solution)/shard_map/ppermute | solution.py:17
  123.8 7.4 %collective-permute-start.19 = (bf16[64,1,2,16]{0,3,2,1:T(8,128)(2,1)S(1)}, bf16[64,1,2,16]{0,3,2,1:T(8,128)(2,1)S(1)}, u32[]{:S(2)}, u32[]{:S(2)}) collective-permute-start(bf16[64,1,2,16]{0,3,2,1:T(8,128)(2,1)S(1)} %bitcast.614), channel_id=1, source_target_pairs={{32,0},{64,32},{96,64},{128,96},{160,128},{192,160},{224,192},{33,... | collective-permute-start | bytes 12296 | tf_op jit(solution)/shard_map/ppermute | solution.py:17
  125.7 6.3 %collective-permute-start.18 = (bf16[64,1,2,16]{0,3,2,1:T(8,128)(2,1)S(1)}, bf16[64,1,2,16]{0,3,2,1:T(8,128)(2,1)S(1)}, u32[]{:S(2)}, u32[]{:S(2)}) collective-permute-start(bf16[64,1,2,16]{0,3,2,1:T(8,128)(2,1)S(1)} %bitcast.615), channel_id=1, source_target_pairs={{0,32},{32,64},{64,96},{96,128},{128,160},{160,192},{192,224},{1,3... | collective-permute-start | bytes 12296 | tf_op jit(solution)/shard_map/ppermute | solution.py:15
  132.0 6.4 %collective-permute-start.20 = (bf16[64,3,1,16]{0,3,2,1:T(8,128)(2,1)S(1)}, bf16[64,3,1,16]{0,3,2,1:T(8,128)(2,1)S(1)}, u32[]{:S(2)}, u32[]{:S(2)}) collective-permute-start(bf16[64,3,1,16]{0,3,2,1:T(8,128)(2,1)S(1)} %get-tuple-element.106), channel_id=1, source_target_pairs={{0,4},{4,8},{8,12},{12,16},{16,20},{20,24},{24,28},{1,5},{5,9},{9,... | collective-permute-start | bytes 18440 | tf_op jit(solution)/shard_map/ppermute | solution.py:15
  136.5 7.1 %collective-permute-start.21 = (bf16[64,3,1,16]{0,3,2,1:T(8,128)(2,1)S(1)}, bf16[64,3,1,16]{0,3,2,1:T(8,128)(2,1)S(1)}, u32[]{:S(2)}, u32[]{:S(2)}) collective-permute-start(bf16[64,3,1,16]{0,3,2,1:T(8,128)(2,1)S(1)} %get-tuple-element.107), channel_id=1, source_target_pairs={{4,0},{8,4},{12,8},{16,12},{20,16},{24,20},{28,24},{5,1},{9,5},{13... | collective-permute-start | bytes 18440 | tf_op jit(solution)/shard_map/ppermute | solution.py:17
  151.6 8.0 %collective-permute-start.24 = (bf16[128,1,4,32]{0,3,2,1:T(8,128)(2,1)S(1)}, bf16[128,1,4,32]{0,3,2,1:T(8,128)(2,1)S(1)}, u32[]{:S(2)}, u32[]{:S(2)}) collective-permute-start(bf16[128,1,4,32]{0,3,2,1:T(8,128)(2,1)S(1)} %get-tuple-element.69), channel_id=1, source_target_pairs={{0,32},{32,64},{64,96},{96,128},{128,160},{160,192},{192,224},{1,3... | collective-permute-start | bytes 98312 | tf_op jit(solution)/shard_map/ppermute | solution.py:15
  157.7 6.8 %collective-permute-start.25 = (bf16[128,1,4,32]{0,3,2,1:T(8,128)(2,1)S(1)}, bf16[128,1,4,32]{0,3,2,1:T(8,128)(2,1)S(1)}, u32[]{:S(2)}, u32[]{:S(2)}) collective-permute-start(bf16[128,1,4,32]{0,3,2,1:T(8,128)(2,1)S(1)} %get-tuple-element.70), channel_id=1, source_target_pairs={{32,0},{64,32},{96,64},{128,96},{160,128},{192,160},{224,192},{33,... | collective-permute-start | bytes 98312 | tf_op jit(solution)/shard_map/ppermute | solution.py:17
  164.5 6.5 %collective-permute-start.26 = (bf16[128,4,1,32]{0,3,2,1:T(8,128)(2,1)S(1)}, bf16[128,4,1,32]{0,3,2,1:T(8,128)(2,1)S(1)}, u32[]{:S(2)}, u32[]{:S(2)}) collective-permute-start(bf16[128,4,1,32]{0,3,2,1:T(8,128)(2,1)S(1)} %get-tuple-element.63), channel_id=1, source_target_pairs={{0,4},{4,8},{8,12},{12,16},{16,20},{20,24},{24,28},{1,5},{5,9},{9,... | collective-permute-start | bytes 98312 | tf_op jit(solution)/shard_map/ppermute | solution.py:15
  169.1 7.3 %collective-permute-start.27 = (bf16[128,4,1,32]{0,3,2,1:T(8,128)(2,1)S(1)}, bf16[128,4,1,32]{0,3,2,1:T(8,128)(2,1)S(1)}, u32[]{:S(2)}, u32[]{:S(2)}) collective-permute-start(bf16[128,4,1,32]{0,3,2,1:T(8,128)(2,1)S(1)} %get-tuple-element.64), channel_id=1, source_target_pairs={{4,0},{8,4},{12,8},{16,12},{20,16},{24,20},{28,24},{5,1},{9,5},{13... | collective-permute-start | bytes 98312 | tf_op jit(solution)/shard_map/ppermute | solution.py:17
  176.5 6.3 %collective-permute-start.28 = (bf16[128,4,6,1]{0,3,2,1:T(2,128)(2,1)S(1)}, bf16[128,4,6,1]{0,3,2,1:T(2,128)(2,1)S(1)}, u32[]{:S(2)}, u32[]{:S(2)}) collective-permute-start(bf16[128,4,6,1]{0,3,2,1:T(2,128)(2,1)S(1)} %get-tuple-element.41), channel_id=1, source_target_pairs={{0,1},{1,2},{2,3},{4,5},{5,6},{6,7},{8,9},{9,10},{10,11},{12,13},{... | collective-permute-start | bytes 18440 | tf_op jit(solution)/shard_map/ppermute | solution.py:15
  185.9 5.7 %collective-permute-start.30 = (bf16[64,1,8,64]{3,0,2,1:T(8,128)(2,1)S(1)}, bf16[64,1,8,64]{3,0,2,1:T(8,128)(2,1)S(1)}, u32[]{:S(2)}, u32[]{:S(2)}) collective-permute-start(bf16[64,1,8,64]{3,0,2,1:T(8,128)(2,1)S(1)} %get-tuple-element.19), channel_id=1, source_target_pairs={{0,32},{32,64},{64,96},{96,128},{128,160},{160,192},{192,224},{1,3... | collective-permute-start | bytes 196616 | tf_op jit(solution)/shard_map/ppermute | solution.py:15
  187.8 7.8 %collective-permute-start.31 = (bf16[64,1,8,64]{3,0,2,1:T(8,128)(2,1)S(1)}, bf16[64,1,8,64]{3,0,2,1:T(8,128)(2,1)S(1)}, u32[]{:S(2)}, u32[]{:S(2)}) collective-permute-start(bf16[64,1,8,64]{3,0,2,1:T(8,128)(2,1)S(1)} %get-tuple-element.20), channel_id=1, source_target_pairs={{32,0},{64,32},{96,64},{128,96},{160,128},{192,160},{224,192},{33,... | collective-permute-start | bytes 196616 | tf_op jit(solution)/shard_map/ppermute | solution.py:17
  195.7 7.2 %collective-permute-start.32 = (bf16[64,6,1,64]{3,0,2,1:T(8,128)(2,1)S(1)}, bf16[64,6,1,64]{3,0,2,1:T(8,128)(2,1)S(1)}, u32[]{:S(2)}, u32[]{:S(2)}) collective-permute-start(bf16[64,6,1,64]{3,0,2,1:T(8,128)(2,1)S(1)} %get-tuple-element.13), channel_id=1, source_target_pairs={{0,4},{4,8},{8,12},{12,16},{16,20},{20,24},{24,28},{1,5},{5,9},{9,... | collective-permute-start | bytes 147464 | tf_op jit(solution)/shard_map/ppermute | solution.py:15
  201.0 8.0 %collective-permute-start.33 = (bf16[64,6,1,64]{3,0,2,1:T(8,128)(2,1)S(1)}, bf16[64,6,1,64]{3,0,2,1:T(8,128)(2,1)S(1)}, u32[]{:S(2)}, u32[]{:S(2)}) collective-permute-start(bf16[64,6,1,64]{3,0,2,1:T(8,128)(2,1)S(1)} %get-tuple-element.14), channel_id=1, source_target_pairs={{4,0},{8,4},{12,8},{16,12},{20,16},{24,20},{28,24},{5,1},{9,5},{13... | collective-permute-start | bytes 147464 | tf_op jit(solution)/shard_map/ppermute | solution.py:17
  211.6 10.5 %collective-permute-start.35 = (bf16[64,6,10,1]{0,1,3,2:T(8,128)(2,1)S(1)}, bf16[64,6,10,1]{0,1,3,2:T(8,128)(2,1)S(1)}, u32[]{:S(2)}, u32[]{:S(2)}) collective-permute-start(bf16[64,6,10,1]{0,1,3,2:T(8,128)(2,1)S(1)} %copy.210), channel_id=1, source_target_pairs={{1,0},{2,1},{3,2},{5,4},{6,5},{7,6},{9,8},{10,9},{11,10},{13,12},{... | collective-permute-start | bytes 23048 | tf_op jit(solution)/shard_map/ppermute | solution.py:17
  260.7 6.0 %collective-permute-start.36 = (bf16[32,1,16,128]{3,0,2,1:T(8,128)(2,1)S(1)}, bf16[32,1,16,128]{3,0,2,1:T(8,128)(2,1)S(1)}, u32[]{:S(2)}, u32[]{:S(2)}) collective-permute-start(bf16[32,1,16,128]{3,0,2,1:T(8,128)(2,1)S(1)} %get-tuple-element.9), channel_id=1, source_target_pairs={{0,32},{32,64},{64,96},{96,128},{128,160},{160,192},{192,224},{1,3... | collective-permute-start | bytes 393224 | tf_op jit(solution)/shard_map/ppermute | solution.py:15
  262.6 7.8 %collective-permute-start.37 = (bf16[32,1,16,128]{3,0,2,1:T(8,128)(2,1)S(1)}, bf16[32,1,16,128]{3,0,2,1:T(8,128)(2,1)S(1)}, u32[]{:S(2)}, u32[]{:S(2)}) collective-permute-start(bf16[32,1,16,128]{3,0,2,1:T(8,128)(2,1)S(1)} %get-tuple-element.10), channel_id=1, source_target_pairs={{32,0},{64,32},{96,64},{128,96},{160,128},{192,160},{224,192},{33,... | collective-permute-start | bytes 393224 | tf_op jit(solution)/shard_map/ppermute | solution.py:17
  270.5 6.1 %collective-permute-start.38 = (bf16[32,10,1,128]{3,0,2,1:T(8,128)(2,1)S(1)}, bf16[32,10,1,128]{3,0,2,1:T(8,128)(2,1)S(1)}, u32[]{:S(2)}, u32[]{:S(2)}) collective-permute-start(bf16[32,10,1,128]{3,0,2,1:T(8,128)(2,1)S(1)} %get-tuple-element.7), channel_id=1, source_target_pairs={{0,4},{4,8},{8,12},{12,16},{16,20},{20,24},{24,28},{1,5},{5,9},{9,... | collective-permute-start | bytes 245768 | tf_op jit(solution)/shard_map/ppermute | solution.py:15
  274.7 7.9 %collective-permute-start.39 = (bf16[32,10,1,128]{3,0,2,1:T(8,128)(2,1)S(1)}, bf16[32,10,1,128]{3,0,2,1:T(8,128)(2,1)S(1)}, u32[]{:S(2)}, u32[]{:S(2)}) collective-permute-start(bf16[32,10,1,128]{3,0,2,1:T(8,128)(2,1)S(1)} %get-tuple-element.8), channel_id=1, source_target_pairs={{4,0},{8,4},{12,8},{16,12},{20,16},{24,20},{28,24},{5,1},{9,5},{13... | collective-permute-start | bytes 245768 | tf_op jit(solution)/shard_map/ppermute | solution.py:17
  289.0 9.5 %collective-permute-start.41 = (bf16[32,10,18,1]{0,2,3,1:T(8,128)(2,1)S(1)}, bf16[32,10,18,1]{0,2,3,1:T(8,128)(2,1)S(1)}, u32[]{:S(2)}, u32[]{:S(2)}) collective-permute-start(bf16[32,10,18,1]{0,2,3,1:T(8,128)(2,1)S(1)} %copy.234), channel_id=1, source_target_pairs={{1,0},{2,1},{3,2},{5,4},{6,5},{7,6},{9,8},{10,9},{11,10},{13,12},{... | collective-permute-start | bytes 34568 | tf_op jit(solution)/shard_map/ppermute | solution.py:17
  (38 other events, 704.6 us)
where the time goes:
time: 334 us; the launch traced here: 328 us
  starting transfers between devices  128 us (38%)
  waiting for transfers between devices  74.7 us (22%)
  other arithmetic  51 us (15%)
  local copies, waits for them, and re-layouts  44.3 us (13%)
  matrix products  28.6 us (9%)
    ppermute x21, starting transfers between devices, extended(): lax.ppermute(tail, axis, [(i, (i + 1) % count) for i in range(ends)])  75.2 us
    ppermute x21, waiting for transfers between devices, extended(): lax.ppermute(head, axis, [((i + 1) % count, i) for i in range(ends)])  68.4 us
    ppermute x21, starting transfers between devices, extended(): lax.ppermute(head, axis, [((i + 1) % count, i) for i in range(ends)])  52.8 us
    concatenate x7, other arithmetic, convolve(): jnp.concatenate([padded[:, :, :, c:c + width] for c in range(3)], axis=0)  40.4 us
    dot_general x60, matrix products, convolve(): jnp.einsum('ok,kdhw->odhw', taps, window, preferred_element_type=jnp.floa...  24.6 us
    reduce_max x3, other arithmetic, pooled(): values.reshape(chans, depth // 2, 2, height // 2, 2, width // 2, 2)  9.31 us
    slice x11, local copies, waits for them, and re-layouts, extended(): lax.slice_in_dim(cells, cells.shape[dim] - width, cells.shape[dim], axis=...  7.25 us
    broadcast_in_dim x4, local copies, waits for them, and re-layouts, upsampled(): jnp.broadcast_to(values[:, :, None, :, None, :, None], (chans, depth, 2,...  6.73 us
  transfers between devices with their start and end apart: 42, of which 23 were waited for; matrix products, arithmetic and copies ran while one was open for 3% of the time, Pallas kernels for 0%

commit v1 on v0

v1 whole, which is shorter than its diff:
```python
import itertools

import jax
import jax.numpy as jnp
from jax import lax
from jax.experimental import pallas as pl
from jax.experimental.pallas import tpu as pltpu
from jax.sharding import PartitionSpec as P

BF16 = jnp.bfloat16
F32 = jnp.float32
STEPS = (-1, 0, 1)
PLANE = [(dz, dy) for dz in STEPS for dy in STEPS]
RING = [step for step in PLANE if step != (0, 0)]
FAR = [(dz, dy) for dz in (-2, -1, 0, 1, 2) for dy in STEPS]


def span(step, size, halo):
    if step == 0:
        return halo, halo, size
    if step > 0:
        return size, 0, halo
    return halo, halo + size, halo


def region(step, size, halo):
    if step == 0:
        return halo, size, 0
    if step < 0:
        return 0, halo, size - halo
    return halo + size, halo, 0


def leaky(total):
    return jnp.maximum(total, 0.1 * total)


def kernel(
    x_ref,
    k0, b0, k1, b1, k2, b2, k3, b3,
    lift2, ku2, c2, lift1, ku1, c1, lift0, kd0, c0,
    out_ref,
    xf, vol, edge0, mine0, stack0,
    zero, edgez, minez,
    pool0, edge1, mine1,
    join1, pool1, join2, pool2, edge2, mine2, join0,
    wa0, wd0, w1, w2, w3, wu2, wu1, wl0,
    pick, grow,
    bias0, bias1, bias2, bias3, off2, off1, off0,
    send_sem, recv_sem,
):
    z, y, x = lax.axis_index("gz"), lax.axis_index("gy"), lax.axis_index("gx")
    nz, ny, nx = lax.axis_size("gz"), lax.axis_size("gy"), lax.axis_size("gx")

    def device(dz, dy, dx):
        return (lax.rem(z + dz + nz, nz), lax.rem(y + dy + ny, ny), lax.rem(x + dx + nx, nx))

    others = [(dz, dy, dx) for dz, dy in FAR for dx in STEPS if (dz, dy, dx) != (0, 0, 0)]
    barrier = pltpu.get_barrier_semaphore()
    for step in others:
        pl.semaphore_signal(
            barrier, inc=1, device_id=device(*step), device_id_type=pl.DeviceIdType.MESH
        )

    count = itertools.count()

    def send(src, dst, step):
        k = next(count)
        copy = pltpu.make_async_remote_copy(
            src_ref=src,
            dst_ref=dst,
            send_sem=send_sem.at[k],
            recv_sem=recv_sem.at[k],
            device_id=device(*step),
            device_id_type=pl.DeviceIdType.MESH,
        )
        copy.start()
        return copy

    def send_rows(buffer, sizes, halo):
        copies = []
        for dz, dy in RING:
            s0, t0, n0 = span(dz, sizes[0], halo)
            s1, t1, n1 = span(dy, sizes[1], halo)
            copies.append(
                send(
                    buffer.at[pl.ds(s0, n0), pl.ds(s1, n1)],
                    buffer.at[pl.ds(t0, n0), pl.ds(t1, n1)],
                    (dz, dy, 0),
                )
            )
        return copies

    def send_edges(mine, edge, steps, reach):
        copies = []
        for dz, dy in steps:
            for dx in (-1, 1):
                side = 0 if dx > 0 else 1
                copies.append(
                    send(mine.at[1 - side], edge.at[side, reach - dz, 1 - dy], (dz, dy, dx))
                )
        return copies

    def wait_recv(copies):
        for copy in copies:
            copy.wait_recv()

    def wait_send(copies):
        for copy in copies:
            copy.wait_send()

    lane = lax.broadcasted_iota(jnp.int32, (1, 128), 1)
    inside_left = (x > 0).astype(jnp.int32)
    inside_right = (x < nx - 1).astype(jnp.int32)

    def within(dz, dy):
        pz, py = z + dz, y + dy
        ok = (pz >= 0) & (pz < nz) & (py >= 0) & (py < ny)
        return ok.astype(jnp.int32)

    for c in range(16):
        xf[pl.ds(c * 128, 128), :] = x_ref[c].reshape(128, 128).astype(F32)

    def to_row(r, _):
        vol[1 + lax.div(r, 16), 1 + lax.rem(r, 16)] = xf[pl.ds(r, 16, stride=128), :].astype(BF16)
        return 0

    lax.fori_loop(0, 128, to_row, 0, unroll=8)
    row_id = lax.broadcasted_iota(jnp.int32, (32, 2048), 0)
    col_id = lax.broadcasted_iota(jnp.int32, (32, 2048), 1)
    wanted = lax.rem(row_id, 16) * 128 + jnp.where(row_id < 16, 0, 127)
    chooser = (col_id == wanted).astype(F32).astype(BF16)
    flat = jnp.concatenate([x_ref[c].reshape(128, 128) for c in range(16)], axis=1)
    ends = lax.dot_general(
        chooser, flat, (((1,), (1,)), ((), ())), preferred_element_type=F32
    ).astype(BF16)
    mine0[0] = ends[:16]
    mine0[1] = ends[16:]

    pl.semaphore_wait(barrier, len(others))
    sent = []
    rows_in = send_rows(vol, (8, 16), 1)
    edges_in = send_edges(mine0, edge0, PLANE, 1)
    sent += rows_in + edges_in

    def column(ref, size):
        a = lax.broadcasted_iota(jnp.int32, (size, size), 0)
        b = lax.broadcasted_iota(jnp.int32, (size, size), 1)
        spread = jnp.broadcast_to(ref[...], (size, size))
        return jnp.sum(jnp.where(a == b, spread, 0.0), axis=1, keepdims=True)

    for ref, target, size, times in (
        (b0, bias0, 16, 4),
        (b1, bias1, 32, 2),
        (b2, bias2, 64, 1),
        (b3, bias3, 128, 1),
        (c2, off2, 64, 1),
        (c1, off1, 32, 2),
        (c0, off0, 16, 4),
    ):
        wide = jnp.broadcast_to(column(ref, size), (size, 128))
        for j in range(times):
            target[pl.ds(j * size, size), :] = wide

    for ref in (wa0, wd0, w1, wu1, wl0):
        ref[...] = jnp.zeros(ref.shape, BF16)
    for a, e, f in itertools.product(range(3), repeat=3):
        tap = (a * 3 + e) * 3 + f
        first, last = k0[tap], kd0[tap]
        for j in range(4):
            at = (a * 6 + e + j) * 48 + f * 16
            wa0[j * 16 : j * 16 + 16, at : at + 16] = first
            at = (a * 6 + e + j) * 96 + f * 16
            wd0[j * 16 : j * 16 + 16, at : at + 16] = last[:, :16]
            wd0[j * 16 : j * 16 + 16, at + 48 : at + 64] = last[:, 16:]
        for j in range(2):
            at = (a * 4 + e + j) * 16
            row = (f * 2 + j) * 32
            w1[row : row + 32, at : at + 16] = k1[tap]
            at = (a * 4 + e + j) * 64
            wu1[row : row + 32, at : at + 64] = ku1[tap]
        at = a * 3 + e
        w2[f * 64 : f * 64 + 64, at * 32 : at * 32 + 32] = k2[tap]
        w3[f * 128 : f * 128 + 128, at * 64 : at * 64 + 64] = k3[tap]
        wu2[f * 64 : f * 64 + 64, at * 128 : at * 128 + 128] = ku2[tap]
    for j in range(2):
        wl0[j * 16 : j * 16 + 16, j * 32 : j * 32 + 32] = lift0[...]

    a = lax.broadcasted_iota(jnp.int32, (128, 256), 0)
    b = lax.broadcasted_iota(jnp.int32, (128, 256), 1)
    cell = lax.rem(b, 128) - 32
    hit = (cell >= 0) & (cell < 64) & (a == 2 * cell + lax.div(b, 128))
    pick[...] = hit.astype(F32).astype(BF16)
    a = lax.broadcasted_iota(jnp.int32, (128, 384), 0)
    b = lax.broadcasted_iota(jnp.int32, (128, 384), 1)
    hit = a == lax.div(lax.rem(b, 128) + lax.div(b, 128) + 1, 2) + 31
    grow[...] = hit.astype(F32).astype(BF16)

    def shifted(src, edge, target, base):
        for dz, dy in PLANE:
            p0, n0, s0 = region(dz, 8, 1)
            p1, n1, s1 = region(dy, 16, 1)
            ok = within(dz, dy)
            ok_left = (ok * inside_left).astype(F32)
            ok_right = (ok * inside_right).astype(F32)
            ok = ok.astype(F32)
            left_edge = edge[0, dz + 1, dy + 1].astype(F32) * ok_left
            right_edge = edge[1, dz + 1, dy + 1].astype(F32) * ok_right

            def body(i, _):
                i0, i1 = lax.div(i, n1), lax.rem(i, n1)
                r = (s0 + i0) * 16 + s1 + i1
                row = src[p0 + i0, p1 + i1].astype(F32)
                if (dz, dy) != (0, 0):
                    row = row * ok
                left = pltpu.roll(left_edge, lax.rem(128 - r, 128), 1)
                right = pltpu.roll(right_edge, 127 - r, 1)
                d, h = base + p0 + i0, base + p1 + i1
                target[d, h, 0:16, :] = jnp.where(lane == 0, left, pltpu.roll(row, 1, 1)).astype(BF16)
                target[d, h, 16:32, :] = row.astype(BF16)
                target[d, h, 32:48, :] = jnp.where(
                    lane == 127, right, pltpu.roll(row, 127, 1)
                ).astype(BF16)
                return 0

            lax.fori_loop(0, n0 * n1, body, 0, unroll=min(4, n0 * n1))

    wait_recv(rows_in + edges_in)
    shifted(vol, edge0, stack0, 0)

    def encode(i, _):
        d, h = lax.div(i, 4) * 2, lax.rem(i, 4) * 4
        cells = [stack0[pl.ds(d + j, 3), pl.ds(h, 6)].reshape(864, 128) for j in range(2)]
        total = jnp.dot(wa0[...], jnp.concatenate(cells, axis=1), preferred_element_type=F32)
        halves = [
            leaky(total[:, j * 128 : j * 128 + 128] + bias0[...]).astype(BF16) for j in range(2)
        ]
        for j in range(2):
            zero[1 + d + j, pl.ds(1 + h, 4)] = halves[j].reshape(4, 16, 128)
        top = jnp.maximum(halves[0], halves[1]).reshape(2, 2, 16, 128)
        top = jnp.maximum(top[:, 0], top[:, 1]).reshape(32, 128)
        both = jnp.dot(top, pick[...], preferred_element_type=F32)
        best = jnp.maximum(both[:, :128], both[:, 128:]).astype(BF16)
        pool0[3 + lax.div(d, 2), pl.ds(3 + lax.div(h, 2), 2)] = best.reshape(2, 16, 128)
        return 0

    lax.fori_loop(0, 16, encode, 0, unroll=2)

    def pack1(r, carry):
        first, last = carry
        row = pool0[3 + lax.div(r, 8), 3 + lax.rem(r, 8)].astype(F32)
        mine = lax.div(lane, 4) == r
        first = jnp.where(mine, pltpu.roll(row, lax.rem(4 * r + 96, 128), 1), first)
        last = jnp.where(mine, pltpu.roll(row, lax.rem(4 * r + 35, 128), 1), last)
        return first, last

    blank = jnp.zeros((16, 128), F32)
    first, last = lax.fori_loop(0, 32, pack1, (blank, blank), unroll=4)
    mine1[0] = first.astype(BF16)
    mine1[1] = last.astype(BF16)
    rows1 = send_rows(pool0, (4, 8), 3)
    edges1 = send_edges(mine1, edge1, PLANE, 1)
    sent += edges1

    def packz(r, carry):
        first, last = carry
        row = zero[1 + lax.div(r, 16), 1 + lax.rem(r, 16)].astype(F32)
        first = jnp.where(lane == r, pltpu.roll(row, r, 1), first)
        last = jnp.where(lane == r, pltpu.roll(row, lax.rem(r + 1, 128), 1), last)
        return first, last

    first, last = lax.fori_loop(0, 128, packz, (blank, blank), unroll=4)
    minez[0] = first.astype(BF16)
    minez[1] = last.astype(BF16)
    rowsz = send_rows(zero, (8, 16), 1)
    edgesz = send_edges(minez, edgez, PLANE, 1)
    sent += rowsz + edgesz

    wait_recv(rows1 + edges1)
    wait_send(rows1)
    for dz, dy in PLANE:
        p0, n0, s0 = region(dz, 4, 3)
        p1, n1, s1 = region(dy, 8, 3)
        ok = within(dz, dy)
        left_edge = edge1[0, dz + 1, dy + 1].astype(F32) * (ok * inside_left).astype(F32)
        right_edge = edge1[1, dz + 1, dy + 1].astype(F32) * (ok * inside_right).astype(F32)
        keep = ok.astype(F32)

        def join_rows(i, _):
            i0, i1 = lax.div(i, n1), lax.rem(i, n1)
            r = (s0 + i0) * 8 + s1 + i1
            row = pool0[p0 + i0, p1 + i1].astype(F32) * keep
            left = pltpu.roll(left_edge, lax.rem(157 - 4 * r, 128), 1)
            right = pltpu.roll(right_edge, lax.rem(224 - 4 * r, 128), 1)
            row = jnp.where((lane >= 29) & (lane < 32), left, row)
            row = jnp.where((lane >= 96) & (lane < 99), right, row)
            pool0[p0 + i0, p1 + i1] = row.astype(BF16)
            return 0

        lax.fori_loop(0, n0 * n1, join_rows, 0, unroll=3 if n0 * n1 == 9 else 4)

    lanes_ok = ((lane >= 32) | (x > 0)) & ((lane < 96) | (x < nx - 1))
    lanes_ok = lanes_ok.astype(jnp.int32)

    def keeps(d, h, depth, height):
        gd, gh = z * depth + d, y * height + h
        ok = (gd >= 0) & (gd < nz * depth) & (gh >= 0) & (gh < ny * height)
        return (lanes_ok * ok.astype(jnp.int32)) > 0

    def combine(total, rows, shift, part):
        cut = slice(part * 128, part * 128 + 128)
        return (
            pltpu.roll(total[:rows, cut], shift, 1)
            + total[rows : 2 * rows, cut]
            + pltpu.roll(total[2 * rows :, cut], 128 - shift, 1)
        )

    def pairs(row, width):
        even = lax.rem(lax.div(lane, width), 2) == 0
        other = jnp.where(even, pltpu.roll(row, 128 - width, 1), pltpu.roll(row, width, 1))
        return jnp.maximum(row, other)

    def second(i, _):
        d, h = lax.div(i, 6) * 2, lax.rem(i, 6) * 2
        cells = [pool0[pl.ds(d + j, 3), pl.ds(h, 4)].reshape(192, 128) for j in range(2)]
        total = jnp.dot(w1[...], jnp.concatenate(cells, axis=1), preferred_element_type=F32)
        best = None
        for j in range(2):
            value = leaky(combine(total, 64, 1, j) + bias1[...])
            for g in range(2):
                row = jnp.where(keeps(d + j - 2, h + g - 2, 4, 8), value[g * 32 : g * 32 + 32], 0.0)
                join1[d + j, h + g, 0:32, :] = row.astype(BF16)
                best = row if best is None else jnp.maximum(best, row)
        pool1[lax.div(d, 2), lax.div(h, 2)] = pairs(best, 1).astype(BF16)
        return 0

    lax.fori_loop(0, 24, second, 0, unroll=2)

    own = (lane >= 32) & (lane < 96)

    def third(h, _):
        cells = [pool1[pl.ds(j, 3), pl.ds(h, 3)].reshape(288, 128) for j in range(2)]
        total = jnp.dot(w2[...], jnp.concatenate(cells, axis=1), preferred_element_type=F32)
        for j in range(2):
            value = leaky(combine(total, 64, 2, j) + bias2[...])
            join2[2 + j, 2 + h, 0:64, :] = jnp.where(own, value, 0.0).astype(BF16)
        return 0

    lax.fori_loop(0, 4, third, 0, unroll=2)
    first = jnp.zeros((64, 128), F32)
    last = jnp.zeros((64, 128), F32)
    for h in range(2):
        best = None
        for j, g in itertools.product(range(2), repeat=2):
            row = join2[2 + j, 2 + 2 * h + g, 0:64, :].astype(F32)
            best = row if best is None else jnp.maximum(best, row)
            r = j * 4 + 2 * h + g
            here = lax.div(lane, 4) == r
            first = jnp.where(here, pltpu.roll(row, (4 * r + 96) % 128, 1), first)
            last = jnp.where(here, pltpu.roll(row, (4 * r + 36) % 128, 1), last)
        best = pairs(best, 2)
        pool2[2, 2 + h] = best.astype(BF16)
        here = lax.div(lane, 8) == 4 + h
        first = jnp.where(here, pltpu.roll(best, 8 * h, 1), first)
        last = jnp.where(here, pltpu.roll(best, 8 * h + 72, 1), last)
    mine2[0] = first.astype(BF16)
    mine2[1] = last.astype(BF16)
    edges2 = send_edges(mine2, edge2, FAR, 2)
    pools2 = [
        send(
            pool2.at[pl.ds(2, 1), pl.ds(2, 2)],
            pool2.at[pl.ds(2 - dz, 1), pl.ds(2 - 2 * dy, 2)],
            (dz, dy, 0),
        )
        for dz, dy in FAR
        if (dz, dy) != (0, 0)
    ]
    rows2 = []
    for dz, dy in RING:
        s0, t0, n0 = span(dz, 2, 2)
        s1, t1, n1 = span(dy, 4, 2)
        rows2.append(
            send(
                join2.at[pl.ds(s0, n0), pl.ds(s1, n1), pl.ds(0, 64)],
                join2.at[pl.ds(t0, n0), pl.ds(t1, n1), pl.ds(0, 64)],
                (dz, dy, 0),
            )
        )
    sent += edges2

    wait_recv(rowsz + edgesz)
    shifted(zero, edgez, join0, 1)

    wait_recv(edges2 + pools2)
    wait_send(pools2)
    for dz, dy in FAR:
        ok = within(dz, dy)
        left_edge = edge2[0, dz + 2, dy + 1].astype(F32) * (ok * inside_left).astype(F32)
        right_edge = edge2[1, dz + 2, dy + 1].astype(F32) * (ok * inside_right).astype(F32)
        keep = ok.astype(F32)
        for r in range(2):
            row = pool2[2 + dz, 2 + 2 * dy + r].astype(F32) * keep
            left = pltpu.roll(left_edge, (24 - 32 - 8 * r) % 128, 1)
            right = pltpu.roll(right_edge, (96 - 32 - 8 * r) % 128, 1)
            row = jnp.where((lane >= 24) & (lane < 32), left, row)
            row = jnp.where((lane >= 96) & (lane < 104), right, row)
            pool2[2 + dz, 2 + 2 * dy + r] = row.astype(BF16)

    def coarsest(i, _):
        d, h = lax.div(i, 2), lax.rem(i, 2) * 2
        cells = [pool2[pl.ds(d, 3), pl.ds(h + j, 3)].reshape(576, 128) for j in range(2)]
        total = jnp.dot(w3[...], jnp.concatenate(cells, axis=1), preferred_element_type=F32)
        low = []
        for j in range(2):
            value = leaky(combine(total, 128, 4, j) + bias3[...])
            low.append(jnp.where(keeps(d - 1, h + j - 1, 1, 2), value, 0.0).astype(BF16))
        up = jnp.dot(lift2[...], jnp.concatenate(low, axis=1), preferred_element_type=F32).astype(BF16)
        for j in range(2):
            for p, q in itertools.product(range(2), repeat=2):
                join2[2 * d + p, 2 * (h + j) + q, 64:128, :] = up[:, j * 128 : j * 128 + 128]
        return 0

    lax.fori_loop(0, 6, coarsest, 0)

    wait_recv(rows2)
    wait_send(rows2)
    for dz, dy in PLANE:
        p0, n0, s0 = region(dz, 2, 2)
        p1, n1, s1 = region(dy, 4, 2)
        ok = within(dz, dy)
        left_edge = edge2[0, dz + 2, dy + 1].astype(F32) * (ok * inside_left).astype(F32)
        right_edge = edge2[1, dz + 2, dy + 1].astype(F32) * (ok * inside_right).astype(F32)
        keep = ok.astype(F32)
        for i0, i1 in itertools.product(range(n0), range(n1)):
            r = (s0 + i0) * 4 + s1 + i1
            row = join2[p0 + i0, p1 + i1, 0:64, :].astype(F32) * keep
            left = pltpu.roll(left_edge, (28 - 4 * r) % 128, 1)
            right = pltpu.roll(right_edge, (96 - 4 * r) % 128, 1)
            row = jnp.where((lane >= 28) & (lane < 32), left, row)
            row = jnp.where((lane >= 96) & (lane < 100), right, row)
            join2[p0 + i0, p1 + i1, 0:64, :] = row.astype(BF16)

    def upper_two(i, _):
        d, h = lax.div(i, 6) * 2, lax.rem(i, 6)
        cells = [join2[pl.ds(d + j, 3), pl.ds(h, 3)].reshape(1152, 128) for j in range(2)]
        total = jnp.dot(wu2[...], jnp.concatenate(cells, axis=1), preferred_element_type=F32)
        low = []
        for j in range(2):
            value = leaky(combine(total, 64, 2, j) + off2[...])
            low.append(jnp.where(keeps(d + j - 1, h - 1, 2, 4), value, 0.0).astype(BF16))
        up = jnp.dot(lift1[...], jnp.concatenate(low, axis=1), preferred_element_type=F32).astype(BF16)
        for j in range(2):
            for p, q in itertools.product(range(2), repeat=2):
                join1[2 * (d + j) + p, 2 * h + q, 32:64, :] = up[:, j * 128 : j * 128 + 128]
        return 0

    lax.fori_loop(0, 12, upper_two, 0)

    def upper_one(i, _):
        d, h = lax.div(i, 5) * 2, lax.rem(i, 5) * 2
        cells = [join1[pl.ds(d + j, 3), pl.ds(h, 4)].reshape(768, 128) for j in range(2)]
        total = jnp.dot(wu1[...], jnp.concatenate(cells, axis=1), preferred_element_type=F32)
        low = []
        for j in range(2):
            value = leaky(combine(total, 64, 1, j) + off1[...])
            kept = [
                jnp.where(keeps(d + j - 1, h + g - 1, 4, 8), value[g * 32 : g * 32 + 32], 0.0)
                for g in range(2)
            ]
            low.append(jnp.concatenate(kept, axis=0).astype(BF16))
        up = jnp.dot(wl0[...], jnp.concatenate(low, axis=1), preferred_element_type=F32).astype(BF16)
        up = jnp.concatenate([up[:, :128], up[:, 128:]], axis=0)
        wide = jnp.dot(up, grow[...], preferred_element_type=F32).astype(BF16)
        for j, g in itertools.product(range(2), repeat=2):
            at = (j * 2 + g) * 16
            three = [wide[at : at + 16, f * 128 : f * 128 + 128] for f in range(3)]
            three = jnp.concatenate(three, axis=0)
            for p, q in itertools.product(range(2), repeat=2):
                join0[2 * (d + j) + p, 2 * (h + g) + q, 48:96, :] = three
        return 0

    lax.fori_loop(0, 15, upper_one, 0)

    def decode(i, _):
        d, h = lax.div(i, 4) * 2, lax.rem(i, 4) * 4
        cells = [join0[pl.ds(d + 1 + j, 3), pl.ds(h + 1, 6)].reshape(1728, 128) for j in range(2)]
        total = jnp.dot(wd0[...], jnp.concatenate(cells, axis=1), preferred_element_type=F32)
        for j in range(2):
            value = leaky(total[:, j * 128 : j * 128 + 128] + off0[...])
            for g in range(4):
                xf[pl.ds((d + j) * 16 + h + g, 16, stride=128), :] = value[g * 16 : g * 16 + 16]
        return 0

    lax.fori_loop(0, 16, decode, 0)
    for c in range(16):
        out_ref[c] = xf[pl.ds(c * 128, 128), :].astype(BF16).reshape(8, 16, 128)

    wait_send(sent)


def taps(weights):
    out, inner = weights.shape[:2]
    return jnp.transpose(weights, (2, 3, 4, 0, 1)).reshape(27, out, inner)


def per_device(
    volume,
    surface_conv,
    surface_bias,
    second_conv,
    second_bias,
    middle_conv,
    middle_bias,
    bottom_conv,
    bottom_bias,
    middle_lift,
    middle_return,
    middle_offset,
    second_lift,
    second_return,
    second_offset,
    surface_lift,
    surface_return,
    surface_offset,
):
    def tile(*shape):
        return pltpu.VMEM(shape, BF16)

    def wide(rows):
        return pltpu.VMEM((rows, 128), F32)

    scratch = [
        wide(2048), tile(10, 18, 16, 128), tile(2, 3, 3, 16, 128), tile(2, 16, 128), tile(10, 18, 48, 128),
        tile(10, 18, 16, 128), tile(2, 3, 3, 16, 128), tile(2, 16, 128),
        tile(10, 14, 16, 128), tile(2, 3, 3, 16, 128), tile(2, 16, 128),
        tile(8, 12, 64, 128), tile(4, 6, 32, 128), tile(6, 8, 128, 128),
        tile(5, 6, 64, 128), tile(2, 5, 3, 64, 128), tile(2, 64, 128), tile(12, 20, 96, 128),
        tile(64, 864), tile(64, 1728), tile(192, 192), tile(192, 288), tile(384, 576),
        tile(192, 1152), tile(192, 768), tile(32, 64),
        tile(128, 256), tile(128, 384),
        wide(64), wide(64), wide(64), wide(128), wide(64), wide(64), wide(64),
        pltpu.SemaphoreType.DMA((130,)), pltpu.SemaphoreType.DMA((130,)),
    ]

    def line(values):
        return values.reshape(1, values.shape[0])

    operands = (
        volume,
        taps(surface_conv), line(surface_bias),
        taps(second_conv), line(second_bias),
        taps(middle_conv), line(middle_bias),
        taps(bottom_conv), line(bottom_bias),
        middle_lift, taps(middle_return), line(middle_offset),
        second_lift, taps(second_return), line(second_offset),
        surface_lift, taps(surface_return), line(surface_offset),
    )
    return pl.pallas_call(
        kernel,
        out_shape=jax.ShapeDtypeStruct(volume.shape, BF16),
        in_specs=[pl.BlockSpec(memory_space=pltpu.VMEM)] * len(operands),
        out_specs=pl.BlockSpec(memory_space=pltpu.VMEM),
        scratch_shapes=scratch,
        compiler_params=pltpu.CompilerParams(
            collective_id=0, has_side_effects=True, vmem_limit_bytes=48 * 2**20
        ),
    )(*operands)


def solution(mesh):
    placed = (P(None, "gz", "gy", "gx"),) + (P(),) * 17
    return jax.shard_map(
        per_device, mesh=mesh, in_specs=placed, out_specs=P(None, "gz", "gy", "gx"), check_vma=False
    )
```

time: 334 us -> 101 us (0.30)
  the two profiles are of different devices: /device:TPU:79 before, /device:TPU:1 now
where the time goes in v1:
time: 101 us
  Pallas kernels  97 us (96%)
  local copies, waits for them, and re-layouts  3.37 us (3%)
    pallas_call x1, Pallas kernels, per_device(): pl.pallas_call(kernel, out_shape=jax.ShapeDtypeStruct(volume.shape, BF16)...  97 us

profile of v1, /device:TPU:1, one launch (start us, length us, event | category | flops | bytes accessed | tf_op | source)
XLA Modules:
  0.0 100.5 jit_solution(3748199721617397075)
XLA Ops:
  0.0 1.1 %copy.19 = bf16[3,3,3,32,16]{4,3,2,1,0:T(8,128)(2,1)S(1)} copy(bf16[3,3,3,32,16]{3,4,2,1,0:T(8,128)(2,1)} %bitcast.41) | data formatting | bytes 55296 | tf_op jit(solution)/shard_map/transpose | solution.py:503
  1.1 0.0 copy-done.16
  1.1 0.0 copy-start.4
  1.1 0.0 copy-start.11
  1.2 0.0 copy-start.12
  1.2 0.0 copy-start.13
  1.2 0.0 copy-start.14
  1.2 0.3 copy.20
  1.5 0.0 copy-done.15
  1.5 0.0 copy-start
  1.5 0.0 copy-start.1
  1.5 0.0 copy-start.2
  1.5 0.0 copy-start.3
  1.5 0.0 copy-start.5
  1.5 0.0 copy-start.6
  1.5 0.0 copy-start.7
  1.5 0.4 copy.21
  2.0 0.0 copy-start.8
  2.0 0.0 copy-start.9
  2.0 0.0 copy-start.10
  2.0 0.0 copy-done.4
  2.0 0.0 copy-done.11
  2.0 0.0 copy-done.12
  2.1 0.4 copy-done
  2.5 0.1 copy-done.1
  2.6 0.1 copy-done.2
  2.7 0.0 copy-done.3
  2.7 0.0 copy-done.5
  2.7 0.0 copy-done.7
  2.8 0.0 copy-done.10
  2.8 97.0 %shard_map.172 = bf16[16,8,16,128]{3,2,1,0:T(8,128)(2,1)S(1)} custom-call(bf16[16,8,16,128]{3,2,1,0:T(8,128)(2,1)S(1)} %copy-done, bf16[27,16,16]{2,1,0:T(8,128)(2,1)S(1)} %bitcast.30, f32[1,16]{1,0:T(1,128)S(1)} %bitcast.32, bf16[27,32,16]{2,1,0:T(8,128)(2,1)S(1)} %bitcast.27, f32[1,32]{1,0:T(1,128)S(1)} %bitcast.33, bf16[27,64,32]{2,1,0:T(8,128)(2,1)S(1)} %bitcast.26, ...), custom_call_target="tpu_custom_call" | custom-call | tf_op jit(solution)/shard_map/pallas_call | solution.py:558
  99.8 0.8 copy.23
  (7 shorter events, 0.0 us)
Async XLA Ops:
  0.0 1.1 %copy-start.16 = (bf16[64,32,3,3,3]{0,1,4,3,2:T(8,128)(2,1)S(1)}, bf16[64,32,3,3,3]{0,1,4,3,2:T(8,128)(2,1)}, u32[]{:S(2)}) copy-start(bf16[64,32,3,3,3]{0,1,4,3,2:T(8,128)(2,1)} %param.23) | copy-start | bytes 331780
  0.0 1.5 %copy-start.15 = (bf16[128,64,3,3,3]{0,1,4,3,2:T(8,128)(2,1)S(1)}, bf16[128,64,3,3,3]{0,1,4,3,2:T(8,128)(2,1)}, u32[]{:S(2)}) copy-start(bf16[128,64,3,3,3]{0,1,4,3,2:T(8,128)(2,1)} %param.25) | copy-start | bytes 1327108
  1.1 0.9 copy-start.4
  1.1 0.9 copy-start.11
  1.2 0.9 copy-start.12
  1.2 0.9 copy-start.13
  1.2 0.9 copy-start.14
  1.5 1.1 %copy-start = (bf16[16,8,16,128]{3,2,1,0:T(8,128)(2,1)S(1)}, bf16[16,8,16,128]{3,2,1,0:T(8,128)(2,1)}, u32[]{:S(2)}) copy-start(bf16[16,8,16,128]{3,2,1,0:T(8,128)(2,1)} %x_ref.1) | copy-start | bytes 1572868
  1.5 1.2 %copy-start.1 = (bf16[64,128,3,3,3]{1,0,4,3,2:T(8,128)(2,1)S(1)}, bf16[64,128,3,3,3]{1,0,4,3,2:T(8,128)(2,1)}, u32[]{:S(2)}) copy-start(bf16[64,128,3,3,3]{1,0,4,3,2:T(8,128)(2,1)} %param.28) | copy-start | bytes 1327108
  1.5 1.2 %copy-start.2 = (bf16[32,64,3,3,3]{1,0,4,3,2:T(8,128)(2,1)S(1)}, bf16[32,64,3,3,3]{1,0,4,3,2:T(8,128)(2,1)}, u32[]{:S(2)}) copy-start(bf16[32,64,3,3,3]{1,0,4,3,2:T(8,128)(2,1)} %param.31) | copy-start | bytes 331780
  1.5 1.2 %copy-start.3 = (bf16[16,16,3,3,3]{1,0,4,3,2:T(8,128)(2,1)S(1)}, bf16[16,16,3,3,3]{1,0,4,3,2:T(8,128)(2,1)}, u32[]{:S(2)}) copy-start(bf16[16,16,3,3,3]{1,0,4,3,2:T(8,128)(2,1)} %param.19) | copy-start | bytes 41476
  1.5 1.2 %copy-start.5 = (bf16[64,128]{1,0:T(8,128)(2,1)S(1)}, bf16[64,128]{1,0:T(8,128)(2,1)}, u32[]{:S(2)}) copy-start(bf16[64,128]{1,0:T(8,128)(2,1)} %lift2.1) | copy-start | bytes 49156
  1.5 1.2 %copy-start.6 = (bf16[32,64]{1,0:T(8,128)(2,1)S(1)}, bf16[32,64]{1,0:T(8,128)(2,1)}, u32[]{:S(2)}) copy-start(bf16[32,64]{1,0:T(8,128)(2,1)} %lift1.1) | copy-start | bytes 12292
  1.5 1.2 %copy-start.7 = (bf16[16,32]{1,0:T(8,128)(2,1)S(1)}, bf16[16,32]{1,0:T(8,128)(2,1)}, u32[]{:S(2)}) copy-start(bf16[16,32]{1,0:T(8,128)(2,1)} %lift0.1) | copy-start | bytes 3076
  2.0 0.8 copy-start.8
  2.0 0.7 copy-start.9
  2.0 0.8 copy-start.10

commit v2 on v1

--- a/solution.py
+++ b/solution.py
@@ -35,20 +35,31 @@
     return jnp.maximum(total, 0.1 * total)
 
 
-def kernel(
-    x_ref,
-    k0, b0, k1, b1, k2, b2, k3, b3,
-    lift2, ku2, c2, lift1, ku1, c1, lift0, kd0, c0,
+def kernel(*refs):
+    sources, refs = refs[:18], refs[18:]
+    out_ref, refs = refs[0], refs[1:]
+    locals_, refs = refs[:18], refs[18:]
+    body(sources, locals_, out_ref, *refs)
+
+
+def body(
+    sources,
+    locals_,
     out_ref,
     xf, vol, edge0, mine0, stack0,
     zero, edgez, minez,
-    pool0, edge1, mine1,
-    join1, pool1, join2, pool2, edge2, mine2, join0,
+    pool0, pair0, edge1, mine1,
+    join1, pool1, join2, pool2, wide2, edge2, mine2, folded2, folded3, join0,
     wa0, wd0, w1, w2, w3, wu2, wu1, wl0,
-    pick, grow,
+    pick, grow, fold2, unfold2, fold3, unfold3, fold_edge, unfold_edge,
     bias0, bias1, bias2, bias3, off2, off1, off0,
-    send_sem, recv_sem,
+    send_sem, recv_sem, load_sem,
 ):
+    (
+        x_ref,
+        k0, b0, k1, b1, k2, b2, k3, b3,
+        lift2, ku2, c2, lift1, ku1, c1, lift0, kd0, c0,
+    ) = locals_
     z, y, x = lax.axis_index("gz"), lax.axis_index("gy"), lax.axis_index("gx")
     nz, ny, nx = lax.axis_size("gz"), lax.axis_size("gy"), lax.axis_size("gx")
 
@@ -61,6 +72,13 @@
         pl.semaphore_signal(
             barrier, inc=1, device_id=device(*step), device_id_type=pl.DeviceIdType.MESH
         )
+
+    loads = [
+        pltpu.make_async_copy(source, local, load_sem.at[k])
+        for k, (source, local) in enumerate(zip(sources, locals_))
+    ]
+    for load in loads:
+        load.start()
 
     count = itertools.count()
 
@@ -77,11 +95,11 @@
         copy.start()
         return copy
 
-    def send_rows(buffer, sizes, halo):
+    def send_rows(buffer, sizes, halos):
         copies = []
         for dz, dy in RING:
-            s0, t0, n0 = span(dz, sizes[0], halo)
-            s1, t1, n1 = span(dy, sizes[1], halo)
+            s0, t0, n0 = span(dz, sizes[0], halos[0])
+            s1, t1, n1 = span(dy, sizes[1], halos[1])
             copies.append(
                 send(
                     buffer.at[pl.ds(s0, n0), pl.ds(s1, n1)],
@@ -118,6 +136,7 @@
         ok = (pz >= 0) & (pz < nz) & (py >= 0) & (py < ny)
         return ok.astype(jnp.int32)
 
+    loads[0].wait()
     for c in range(16):
         xf[pl.ds(c * 128, 128), :] = x_ref[c].reshape(128, 128).astype(F32)
 
@@ -139,9 +158,12 @@
 
     pl.semaphore_wait(barrier, len(others))
     sent = []
-    rows_in = send_rows(vol, (8, 16), 1)
+    rows_in = send_rows(vol, (8, 16), (1, 1))
     edges_in = send_edges(mine0, edge0, PLANE, 1)
     sent += rows_in + edges_in
+
+    for load in loads[1:]:
+        load.wait()
 
     def column(ref, size):
         a = lax.broadcasted_iota(jnp.int32, (size, size), 0)
@@ -162,7 +184,7 @@
         for j in range(times):
             target[pl.ds(j * size, size), :] = wide
 
-    for ref in (wa0, wd0, w1, wu1, wl0):
+    for ref in (wa0, wd0, wu1, wl0):
         ref[...] = jnp.zeros(ref.shape, BF16)
     for a, e, f in itertools.product(range(3), repeat=3):
         tap = (a * 3 + e) * 3 + f
@@ -174,27 +196,69 @@
             wd0[j * 16 : j * 16 + 16, at : at + 16] = last[:, :16]
             wd0[j * 16 : j * 16 + 16, at + 48 : at + 64] = last[:, 16:]
         for j in range(2):
-            at = (a * 4 + e + j) * 16
             row = (f * 2 + j) * 32
-            w1[row : row + 32, at : at + 16] = k1[tap]
             at = (a * 4 + e + j) * 64
             wu1[row : row + 32, at : at + 64] = ku1[tap]
         at = a * 3 + e
-        w2[f * 64 : f * 64 + 64, at * 32 : at * 32 + 32] = k2[tap]
-        w3[f * 128 : f * 128 + 128, at * 64 : at * 64 + 64] = k3[tap]
         wu2[f * 64 : f * 64 + 64, at * 128 : at * 128 + 128] = ku2[tap]
+
+    def turned(pieces, size):
+        a = lax.broadcasted_iota(jnp.int32, (size, size), 0)
+        b = lax.broadcasted_iota(jnp.int32, (size, size), 1)
+        return lax.dot_general(
+            (a == b).astype(F32).astype(BF16),
+            jnp.concatenate(pieces, axis=0),
+            (((1,), (1,)), ((), ())),
+            preferred_element_type=F32,
+        ).astype(BF16)
+
+    gap = jnp.zeros((16, 32), BF16)
+    for f in range(3):
+        for j in range(2):
+            pieces = [
+                k1[(a * 3 + g - j) * 3 + f] if 0 <= g - j < 3 else gap
+                for a, g in itertools.product(range(3), range(4))
+            ]
+            row = (f * 2 + j) * 32
+            w1[row : row + 32, :] = turned(pieces, 32)
+        w2[f * 64 : f * 64 + 64, :] = turned([k2[at * 3 + f] for at in range(9)], 64)
+        w3[f * 128 : f * 128 + 128, :] = turned([k3[at * 3 + f] for at in range(9)], 128)
     for j in range(2):
         wl0[j * 16 : j * 16 + 16, j * 32 : j * 32 + 32] = lift0[...]
 
-    a = lax.broadcasted_iota(jnp.int32, (128, 256), 0)
-    b = lax.broadcasted_iota(jnp.int32, (128, 256), 1)
-    cell = lax.rem(b, 128) - 32
-    hit = (cell >= 0) & (cell < 64) & (a == 2 * cell + lax.div(b, 128))
-    pick[...] = hit.astype(F32).astype(BF16)
-    a = lax.broadcasted_iota(jnp.int32, (128, 384), 0)
-    b = lax.broadcasted_iota(jnp.int32, (128, 384), 1)
-    hit = a == lax.div(lax.rem(b, 128) + lax.div(b, 128) + 1, 2) + 31
-    grow[...] = hit.astype(F32).astype(BF16)
+    def selector(target, rule):
+        a = lax.broadcasted_iota(jnp.int32, target.shape, 0)
+        b = lax.broadcasted_iota(jnp.int32, target.shape, 1)
+        target[...] = rule(a, b).astype(F32).astype(BF16)
+
+    def pick_rule(a, b):
+        cell = (b & 127) - 32
+        return (cell >= 0) & (cell < 64) & (a == 2 * cell + (b >> 7))
+
+    def rule2(tall, flat, spread):
+        q, at = tall >> 7, (tall & 127) - 32
+        w = flat & 31
+        return (q == (flat >> 5)) & (at >= 2 * w) & (at < 2 * w + spread)
+
+    def rule3(tall, flat, spread):
+        r, q, at = tall >> 9, (tall >> 7) & 3, (tall & 127) - 32
+        w = flat & 15
+        return (q == (flat >> 5)) & (r == ((flat >> 4) & 1)) & (at >= 4 * w) & (at < 4 * w + spread)
+
+    def rule_edge(tall, flat, spread):
+        q, at, m = tall >> 7, tall & 127, flat & 31
+        size = jnp.where(m < 16, 2, 4)
+        start = jnp.where(m < 16, 2 * m, 4 * m - 32)
+        return (q == (flat >> 5)) & (m < 20) & (at >= start) & (at < start + (size if spread else 1))
+
+    selector(pick, pick_rule)
+    selector(grow, lambda a, b: a == (((b & 127) + (b >> 7) + 1) >> 1) + 31)
+    selector(fold2, lambda a, b: rule2(a, b, 1))
+    selector(unfold2, lambda a, b: rule2(b, a, 2))
+    selector(fold3, lambda a, b: rule3(a, b, 1))
+    selector(unfold3, lambda a, b: rule3(b, a, 4))
+    selector(fold_edge, lambda a, b: rule_edge(a, b, False))
+    selector(unfold_edge, lambda a, b: rule_edge(b, a, True))
 
     def shifted(src, edge, target, base):
         for dz, dy in PLANE:
@@ -240,8 +304,11 @@
         top = jnp.maximum(halves[0], halves[1]).reshape(2, 2, 16, 128)
         top = jnp.maximum(top[:, 0], top[:, 1]).reshape(32, 128)
         both = jnp.dot(top, pick[...], preferred_element_type=F32)
-        best = jnp.maximum(both[:, :128], both[:, 128:]).astype(BF16)
-        pool0[3 + lax.div(d, 2), pl.ds(3 + lax.div(h, 2), 2)] = best.reshape(2, 16, 128)
+        best = jnp.maximum(both[:, :128], both[:, 128:])
+        pool0[3 + lax.div(d, 2), pl.ds(3 + lax.div(h, 2), 2)] = best.astype(BF16).reshape(2, 16, 128)
+        pair0[3 + lax.div(d, 2), 2 + lax.div(h, 4)] = (
+            best[:16] + pltpu.roll(best[16:], 64, 1)
+        ).astype(BF16)
         return 0
 
     lax.fori_loop(0, 16, encode, 0, unroll=2)
@@ -258,9 +325,11 @@
     first, last = lax.fori_loop(0, 32, pack1, (blank, blank), unroll=4)
     mine1[0] = first.astype(BF16)
     mine1[1] = last.astype(BF16)
-    rows1 = send_rows(pool0, (4, 8), 3)
+    rows1 = send_rows(pair0, (4, 4), (3, 2))
     edges1 = send_edges(mine1, edge1, PLANE, 1)
-    sent += edges1
+    sent += rows1 + edges1
+
+    wait_recv(rows1 + edges1)
 
     def packz(r, carry):
         first, last = carry
@@ -272,12 +341,11 @@
     first, last = lax.fori_loop(0, 128, packz, (blank, blank), unroll=4)
     minez[0] = first.astype(BF16)
     minez[1] = last.astype(BF16)
-    rowsz = send_rows(zero, (8, 16), 1)
+    rowsz = send_rows(zero, (8, 16), (1, 1))
     edgesz = send_edges(minez, edgez, PLANE, 1)
     sent += rowsz + edgesz
 
-    wait_recv(rows1 + edges1)
-    wait_send(rows1)
+    own = (lane >= 32) & (lane < 96)
     for dz, dy in PLANE:
         p0, n0, s0 = region(dz, 4, 3)
         p1, n1, s1 = region(dy, 8, 3)
@@ -289,7 +357,12 @@
         def join_rows(i, _):
             i0, i1 = lax.div(i, n1), lax.rem(i, n1)
             r = (s0 + i0) * 8 + s1 + i1
-            row = pool0[p0 + i0, p1 + i1].astype(F32) * keep
+            if (dz, dy) == (0, 0):
+                row = pool0[p0 + i0, p1 + i1].astype(F32)
+            else:
+                at = p1 + i1 + 1
+                row = pair0[p0 + i0, lax.div(at, 2)].astype(F32) * keep
+                row = jnp.where(own, pltpu.roll(row, 64 * lax.rem(at, 2), 1), 0.0)
             left = pltpu.roll(left_edge, lax.rem(157 - 4 * r, 128), 1)
             right = pltpu.roll(right_edge, lax.rem(224 - 4 * r, 128), 1)
             row = jnp.where((lane >= 29) & (lane < 32), left, row)
@@ -336,7 +409,6 @@
 
     lax.fori_loop(0, 24, second, 0, unroll=2)
 
-    own = (lane >= 32) & (lane < 96)
 
     def third(h, _):
         cells = [pool1[pl.ds(j, 3), pl.ds(h, 3)].reshape(288, 128) for j in range(2)]
@@ -363,40 +435,61 @@
         here = lax.div(lane, 8) == 4 + h
         first = jnp.where(here, pltpu.roll(best, 8 * h, 1), first)
         last = jnp.where(here, pltpu.roll(best, 8 * h + 72, 1), last)
-    mine2[0] = first.astype(BF16)
-    mine2[1] = last.astype(BF16)
+    def fold(rows, groups, matrix):
+        size = rows[0].shape[0] // groups
+        pieces = [row[q * size : q * size + size] for q in range(groups) for row in rows]
+        return jnp.dot(
+            jnp.concatenate(pieces, axis=1), matrix[...], preferred_element_type=F32
+        ).astype(BF16)
+
+    mine2[0] = fold([first.astype(BF16)], 4, fold_edge)
+    mine2[1] = fold([last.astype(BF16)], 4, fold_edge)
+    pieces = [pool2[2, 2 + r][q * 16 : q * 16 + 16] for r in range(2) for q in range(4)]
+    folded3[2, 1] = jnp.dot(
+        jnp.concatenate(pieces, axis=1), fold3[...], preferred_element_type=F32
+    ).astype(BF16)
     edges2 = send_edges(mine2, edge2, FAR, 2)
     pools2 = [
-        send(
-            pool2.at[pl.ds(2, 1), pl.ds(2, 2)],
-            pool2.at[pl.ds(2 - dz, 1), pl.ds(2 - 2 * dy, 2)],
-            (dz, dy, 0),
-        )
+        send(folded3.at[2, 1], folded3.at[2 - dz, 1 - dy], (dz, dy, 0))
         for dz, dy in FAR
         if (dz, dy) != (0, 0)
     ]
-    rows2 = []
-    for dz, dy in RING:
-        s0, t0, n0 = span(dz, 2, 2)
-        s1, t1, n1 = span(dy, 4, 2)
-        rows2.append(
-            send(
-                join2.at[pl.ds(s0, n0), pl.ds(s1, n1), pl.ds(0, 64)],
-                join2.at[pl.ds(t0, n0), pl.ds(t1, n1), pl.ds(0, 64)],
-                (dz, dy, 0),
-            )
-        )
+    for j, g in itertools.product(range(2), repeat=2):
+        rows = [join2[2 + j, 2 + 2 * g + p, 0:64, :] for p in range(2)]
+        folded2[2 + j, 1 + g] = fold(rows, 2, fold2)
+    rows2 = send_rows(folded2, (2, 2), (2, 1))
+    sent += pools2 + rows2
     sent += edges2
 
     wait_recv(rowsz + edgesz)
     shifted(zero, edgez, join0, 1)
 
     wait_recv(edges2 + pools2)
-    wait_send(pools2)
+    for side in range(2):
+        for dz in range(5):
+            parts = jnp.dot(
+                edge2[side, dz].reshape(48, 128), unfold_edge[...], preferred_element_type=F32
+            ).astype(BF16)
+            for q in range(4):
+                wide2[side, dz, :, q * 16 : q * 16 + 16, :] = parts[
+                    :, q * 128 : q * 128 + 128
+                ].reshape(3, 16, 128)
+    for dz in range(-2, 3):
+        if dz != 0:
+            tiles, steps = folded3[2 + dz].reshape(48, 128), STEPS
+        else:
+            tiles, steps = jnp.concatenate([folded3[2, 0], folded3[2, 2]], axis=0), (-1, 1)
+        parts = jnp.dot(tiles, unfold3[...], preferred_element_type=F32).astype(BF16)
+        for k, dy in enumerate(steps):
+            for r, q in itertools.product(range(2), range(4)):
+                at = (r * 4 + q) * 128
+                pool2[2 + dz, 2 + 2 * dy + r, q * 16 : q * 16 + 16, :] = parts[
+                    k * 16 : k * 16 + 16, at : at + 128
+                ]
     for dz, dy in FAR:
         ok = within(dz, dy)
-        left_edge = edge2[0, dz + 2, dy + 1].astype(F32) * (ok * inside_left).astype(F32)
-        right_edge = edge2[1, dz + 2, dy + 1].astype(F32) * (ok * inside_right).astype(F32)
+        left_edge = wide2[0, dz + 2, dy + 1].astype(F32) * (ok * inside_left).astype(F32)
+        right_edge = wide2[1, dz + 2, dy + 1].astype(F32) * (ok * inside_right).astype(F32)
         keep = ok.astype(F32)
         for r in range(2):
             row = pool2[2 + dz, 2 + 2 * dy + r].astype(F32) * keep
@@ -420,16 +513,27 @@
                 join2[2 * d + p, 2 * (h + j) + q, 64:128, :] = up[:, j * 128 : j * 128 + 128]
         return 0
 
-    lax.fori_loop(0, 6, coarsest, 0)
+    lax.fori_loop(0, 6, coarsest, 0, unroll=3)
 
     wait_recv(rows2)
-    wait_send(rows2)
+    for d in range(6):
+        near = d in (2, 3)
+        tiles = [folded2[d, g] for g in ((0, 3) if near else range(4))]
+        parts = jnp.dot(
+            jnp.concatenate(tiles, axis=0), unfold2[...], preferred_element_type=F32
+        ).astype(BF16)
+        for k, g in enumerate((0, 3) if near else range(4)):
+            for q, p in itertools.product(range(2), repeat=2):
+                at = (q * 2 + p) * 128
+                join2[d, 2 * g + p, q * 32 : q * 32 + 32, :] = parts[
+                    k * 32 : k * 32 + 32, at : at + 128
+                ]
     for dz, dy in PLANE:
         p0, n0, s0 = region(dz, 2, 2)
         p1, n1, s1 = region(dy, 4, 2)
         ok = within(dz, dy)
-        left_edge = edge2[0, dz + 2, dy + 1].astype(F32) * (ok * inside_left).astype(F32)
-        right_edge = edge2[1, dz + 2, dy + 1].astype(F32) * (ok * inside_right).astype(F32)
+        left_edge = wide2[0, dz + 2, dy + 1].astype(F32) * (ok * inside_left).astype(F32)
+        right_edge = wide2[1, dz + 2, dy + 1].astype(F32) * (ok * inside_right).astype(F32)
         keep = ok.astype(F32)
         for i0, i1 in itertools.product(range(n0), range(n1)):
             r = (s0 + i0) * 4 + s1 + i1
@@ -454,7 +558,7 @@
                 join1[2 * (d + j) + p, 2 * h + q, 32:64, :] = up[:, j * 128 : j * 128 + 128]
         return 0
 
-    lax.fori_loop(0, 12, upper_two, 0)
+    lax.fori_loop(0, 12, upper_two, 0, unroll=3)
 
     def upper_one(i, _):
         d, h = lax.div(i, 5) * 2, lax.rem(i, 5) * 2
@@ -479,7 +583,7 @@
                 join0[2 * (d + j) + p, 2 * (h + g) + q, 48:96, :] = three
         return 0
 
-    lax.fori_loop(0, 15, upper_one, 0)
+    lax.fori_loop(0, 15, upper_one, 0, unroll=3)
 
     def decode(i, _):
         d, h = lax.div(i, 4) * 2, lax.rem(i, 4) * 4
@@ -491,7 +595,7 @@
                 xf[pl.ds((d + j) * 16 + h + g, 16, stride=128), :] = value[g * 16 : g * 16 + 16]
         return 0
 
-    lax.fori_loop(0, 16, decode, 0)
+    lax.fori_loop(0, 16, decode, 0, unroll=2)
     for c in range(16):
         out_ref[c] = xf[pl.ds(c * 128, 128), :].astype(BF16).reshape(8, 16, 128)
 
@@ -501,6 +605,11 @@
 def taps(weights):
     out, inner = weights.shape[:2]
     return jnp.transpose(weights, (2, 3, 4, 0, 1)).reshape(27, out, inner)
+
+
+def turned_taps(weights):
+    out, inner = weights.shape[:2]
+    return jnp.transpose(weights, (2, 3, 4, 1, 0)).reshape(27, inner, out)
 
 
 def per_device(
@@ -532,14 +641,16 @@
     scratch = [
         wide(2048), tile(10, 18, 16, 128), tile(2, 3, 3, 16, 128), tile(2, 16, 128), tile(10, 18, 48, 128),
         tile(10, 18, 16, 128), tile(2, 3, 3, 16, 128), tile(2, 16, 128),
-        tile(10, 14, 16, 128), tile(2, 3, 3, 16, 128), tile(2, 16, 128),
+        tile(10, 14, 16, 128), tile(10, 8, 16, 128), tile(2, 3, 3, 16, 128), tile(2, 16, 128),
         tile(8, 12, 64, 128), tile(4, 6, 32, 128), tile(6, 8, 128, 128),
-        tile(5, 6, 64, 128), tile(2, 5, 3, 64, 128), tile(2, 64, 128), tile(12, 20, 96, 128),
+        tile(5, 6, 64, 128), tile(2, 5, 3, 64, 128), tile(2, 5, 3, 16, 128), tile(2, 16, 128),
+        tile(6, 4, 32, 128), tile(5, 3, 16, 128), tile(12, 20, 96, 128),
         tile(64, 864), tile(64, 1728), tile(192, 192), tile(192, 288), tile(384, 576),
         tile(192, 1152), tile(192, 768), tile(32, 64),
         tile(128, 256), tile(128, 384),
+        tile(512, 128), tile(128, 512), tile(1024, 128), tile(128, 1024), tile(512, 128), tile(128, 512),
         wide(64), wide(64), wide(64), wide(128), wide(64), wide(64), wide(64),
-        pltpu.SemaphoreType.DMA((130,)), pltpu.SemaphoreType.DMA((130,)),
+        pltpu.SemaphoreType.DMA((130,)), pltpu.SemaphoreType.DMA((130,)), pltpu.SemaphoreType.DMA((18,)),
     ]
 
     def line(values):
@@ -548,9 +659,9 @@
     operands = (
         volume,
         taps(surface_conv), line(surface_bias),
-        taps(second_conv), line(second_bias),
-        taps(middle_conv), line(middle_bias),
-        taps(bottom_conv), line(bottom_bias),
+        turned_taps(second_conv), line(second_bias),
+        turned_taps(middle_conv), line(middle_bias),
+        turned_taps(bottom_conv), line(bottom_bias),
         middle_lift, taps(middle_return), line(middle_offset),
         second_lift, taps(second_return), line(second_offset),
         surface_lift, taps(surface_return), line(surface_offset),
@@ -558,11 +669,11 @@
     return pl.pallas_call(
         kernel,
         out_shape=jax.ShapeDtypeStruct(volume.shape, BF16),
-        in_specs=[pl.BlockSpec(memory_space=pltpu.VMEM)] * len(operands),
+        in_specs=[pl.BlockSpec(memory_space=pltpu.HBM)] * len(operands),
         out_specs=pl.BlockSpec(memory_space=pltpu.VMEM),
-        scratch_shapes=scratch,
+        scratch_shapes=[pltpu.VMEM(value.shape, value.dtype) for value in operands] + scratch,
         compiler_params=pltpu.CompilerParams(
-            collective_id=0, has_side_effects=True, vmem_limit_bytes=48 * 2**20
+            collective_id=0, has_side_effects=True, vmem_limit_bytes=60 * 2**20
         ),
     )(*operands)
 

time: 101 us -> 81.5 us (0.81)
  Pallas kernels: 97 us -> 79.5 us
  local copies, waits for them, and re-layouts: 3.37 us -> 1.89 us
    pallas_call x1, Pallas kernels: 97 us -> 79.5 us  [per_device(): pl.pallas_call(kernel, out_shape=jax.ShapeDtypeStruct(volume.shape, BF16)...]
    transpose x3 -> x0, local copies, waits for them, and re-layouts: 1.8 us -> none  [taps(): return jnp.transpose(weights, (2, 3, 4, 0, 1)).reshape(27, out, inner)]
where the time goes in v2:
time: 81.5 us; the launch traced here: 81.4 us
  Pallas kernels  79.5 us (98%)
  local copies, waits for them, and re-layouts  1.89 us (2%)
    pallas_call x1, Pallas kernels, per_device(): pl.pallas_call(kernel, out_shape=jax.ShapeDtypeStruct(volume.shape, BF16)...  79.5 us
    unnamed x1, local copies, waits for them, and re-layouts  1.89 us

profile of v2, /device:TPU:1, one launch (start us, length us, event | category | flops | bytes accessed | tf_op | source)
XLA Modules:
  0.0 81.4 jit_solution(1911957471866619825)
XLA Ops:
  0.0 79.5 %shard_map.172 = bf16[16,8,16,128]{3,2,1,0:T(8,128)(2,1)} custom-call(bf16[16,8,16,128]{3,2,1,0:T(8,128)(2,1)} %refs_0_.1, bf16[27,16,16]{2,1,0:T(8,128)(2,1)} %bitcast.32, f32[1,16]{1,0:T(1,128)} %bitcast.35, bf16[27,16,32]{2,1,0:T(8,128)(2,1)} %bitcast.33, f32[1,32]{1,0:T(1,128)} %bitcast.36, bf16[27,32,64]{2,1,0:T(8,128)(2,1)} %bitcast.30, ...), custom_call_target="tpu_custom_call" | custom-call | tf_op jit(solution)/shard_map/pallas_call | solution.py:669
  79.5 1.9 %copy.20 = bf16[16,8,16,128]{3,2,1,0:T(8,128)(2,1)} copy(bf16[16,8,16,128]{3,2,1,0:T(8,128)(2,1)} %shard_map.172) | data formatting | bytes 1048576

commit v3 on v2

--- a/solution.py
+++ b/solution.py
@@ -48,9 +48,9 @@
     out_ref,
     xf, vol, edge0, mine0, stack0,
     zero, edgez, minez,
-    pool0, pair0, edge1, mine1,
-    join1, pool1, join2, pool2, wide2, edge2, mine2, folded2, folded3, join0,
-    wa0, wd0, w1, w2, w3, wu2, wu1, wl0,
+    top0, pool0, pair0, edge1, mine1,
+    skip1, low2, lifted1, pool1, skip2, low3, up2, pool2, wide2, edge2, mine2, folded2, folded3, low1, lifted0, part0, part1,
+    wa0, wds, wdl, w1, w2, w3, wu2, wus, wul, wl0,
     pick, grow, fold2, unfold2, fold3, unfold3, fold_edge, unfold_edge,
     bias0, bias1, bias2, bias3, off2, off1, off0,
     send_sem, recv_sem, load_sem,
@@ -66,7 +66,8 @@
     def device(dz, dy, dx):
         return (lax.rem(z + dz + nz, nz), lax.rem(y + dy + ny, ny), lax.rem(x + dx + nx, nx))
 
-    others = [(dz, dy, dx) for dz, dy in FAR for dx in STEPS if (dz, dy, dx) != (0, 0, 0)]
+    beyond = [step for step in FAR if step not in PLANE]
+    others = [(*step, dx) for step in PLANE + beyond for dx in STEPS if (*step, dx) != (0, 0, 0)]
     barrier = pltpu.get_barrier_semaphore()
     for step in others:
         pl.semaphore_signal(
@@ -184,21 +185,124 @@
         for j in range(times):
             target[pl.ds(j * size, size), :] = wide
 
-    for ref in (wa0, wd0, wu1, wl0):
+    wa0[...] = jnp.zeros(wa0.shape, BF16)
+    for a, e, f in itertools.product(range(3), repeat=3):
+        first = k0[(a * 3 + e) * 3 + f]
+        for j in range(4):
+            at = (a * 6 + e + j) * 48 + f * 16
+            wa0[j * 16 : j * 16 + 16, at : at + 16] = first
+
+    def selector(target, rule):
+        a = lax.broadcasted_iota(jnp.int32, target.shape, 0)
+        b = lax.broadcasted_iota(jnp.int32, target.shape, 1)
+        target[...] = rule(a, b).astype(F32).astype(BF16)
+
+    def pick_rule(a, b):
+        cell = (b & 127) - 32
+        return (cell >= 0) & (cell < 64) & (a == 2 * cell + (b >> 7))
+
+    def rule2(tall, flat, spread):
+        q, at = tall >> 7, (tall & 127) - 32
+        w = flat & 31
+        return (q == (flat >> 5)) & (at >= 2 * w) & (at < 2 * w + spread)
+
+    def rule3(tall, flat, spread):
+        r, q, at = tall >> 9, (tall >> 7) & 3, (tall & 127) - 32
+        w = flat & 15
+        return (q == (flat >> 5)) & (r == ((flat >> 4) & 1)) & (at >= 4 * w) & (at < 4 * w + spread)
+
+    def rule_edge(tall, flat, spread):
+        q, at, m = tall >> 7, tall & 127, flat & 31
+        size = jnp.where(m < 16, 2, 4)
+        start = jnp.where(m < 16, 2 * m, 4 * m - 32)
+        return (q == (flat >> 5)) & (m < 20) & (at >= start) & (at < start + (size if spread else 1))
+
+    selector(pick, pick_rule)
+    def shifted(src, edge, target):
+        for dz, dy in PLANE:
+            p0, n0, s0 = region(dz, 8, 1)
+            p1, n1, s1 = region(dy, 16, 1)
+            ok = within(dz, dy)
+            ok_left = (ok * inside_left).astype(F32)
+            ok_right = (ok * inside_right).astype(F32)
+            ok = ok.astype(F32)
+            left_edge = edge[0, dz + 1, dy + 1].astype(F32) * ok_left
+            right_edge = edge[1, dz + 1, dy + 1].astype(F32) * ok_right
+
+            def body(i, _):
+                i0, i1 = lax.div(i, n1), lax.rem(i, n1)
+                r = (s0 + i0) * 16 + s1 + i1
+                row = src[p0 + i0, p1 + i1].astype(F32)
+                if (dz, dy) != (0, 0):
+                    row = row * ok
+                left = pltpu.roll(left_edge, lax.rem(128 - r, 128), 1)
+                right = pltpu.roll(right_edge, 127 - r, 1)
+                d, h = p0 + i0, p1 + i1
+                target[d, h, 0:16, :] = jnp.where(lane == 0, left, pltpu.roll(row, 1, 1)).astype(BF16)
+                target[d, h, 16:32, :] = row.astype(BF16)
+                target[d, h, 32:48, :] = jnp.where(
+                    lane == 127, right, pltpu.roll(row, 127, 1)
+                ).astype(BF16)
+                return 0
+
+            lax.fori_loop(0, n0 * n1, body, 0, unroll=min(8, n0 * n1))
+
+    wait_recv(rows_in + edges_in)
+    shifted(vol, edge0, stack0)
+
+    def encode(i, _):
+        d, h = lax.div(i, 4) * 2, lax.rem(i, 4) * 4
+        cells = [stack0[pl.ds(d + j, 3), pl.ds(h, 6)].reshape(864, 128) for j in range(2)]
+        total = jnp.dot(wa0[...], jnp.concatenate(cells, axis=1), preferred_element_type=F32)
+        halves = [
+            leaky(total[:, j * 128 : j * 128 + 128] + bias0[...]).astype(BF16) for j in range(2)
+        ]
+        for j in range(2):
+            zero[1 + d + j, pl.ds(1 + h, 4)] = halves[j].reshape(4, 16, 128)
+        top = jnp.maximum(halves[0], halves[1]).reshape(2, 2, 16, 128)
+        top = jnp.maximum(top[:, 0], top[:, 1])
+        top0[lax.div(d, 2), pl.ds(lax.div(h, 2), 2)] = top
+        return 0
+
+    lax.fori_loop(0, 16, encode, 0, unroll=4)
+    for d in range(4):
+        both = jnp.dot(top0[d].reshape(128, 128), pick[...], preferred_element_type=F32)
+        best = jnp.maximum(both[:, :128], both[:, 128:])
+        pool0[3 + d, 3:11] = best.astype(BF16).reshape(8, 16, 128)
+        best = best.reshape(4, 2, 16, 128)
+        odd = pltpu.roll(best[:, 1].reshape(64, 128), 64, 1)
+        pair0[3 + d, 2:6] = (best[:, 0].reshape(64, 128) + odd).astype(BF16).reshape(4, 16, 128)
+
+    def pack1(r, carry):
+        first, last = carry
+        row = pool0[3 + lax.div(r, 8), 3 + lax.rem(r, 8)].astype(F32)
+        mine = lax.div(lane, 4) == r
+        first = jnp.where(mine, pltpu.roll(row, lax.rem(4 * r + 96, 128), 1), first)
+        last = jnp.where(mine, pltpu.roll(row, lax.rem(4 * r + 35, 128), 1), last)
+        return first, last
+
+    blank = jnp.zeros((16, 128), F32)
+    first, last = lax.fori_loop(0, 32, pack1, (blank, blank), unroll=8)
+    mine1[0] = first.astype(BF16)
+    mine1[1] = last.astype(BF16)
+    rows1 = send_rows(pair0, (4, 4), (3, 2))
+    edges1 = send_edges(mine1, edge1, PLANE, 1)
+    sent += rows1 + edges1
+
+    for ref in (wds, wdl, wus, wul, wl0):
         ref[...] = jnp.zeros(ref.shape, BF16)
     for a, e, f in itertools.product(range(3), repeat=3):
         tap = (a * 3 + e) * 3 + f
-        first, last = k0[tap], kd0[tap]
+        last = kd0[tap]
         for j in range(4):
             at = (a * 6 + e + j) * 48 + f * 16
-            wa0[j * 16 : j * 16 + 16, at : at + 16] = first
-            at = (a * 6 + e + j) * 96 + f * 16
-            wd0[j * 16 : j * 16 + 16, at : at + 16] = last[:, :16]
-            wd0[j * 16 : j * 16 + 16, at + 48 : at + 64] = last[:, 16:]
+            wds[j * 16 : j * 16 + 16, at : at + 16] = last[:, :16]
+            wdl[j * 16 : j * 16 + 16, at : at + 16] = last[:, 16:]
         for j in range(2):
             row = (f * 2 + j) * 32
-            at = (a * 4 + e + j) * 64
-            wu1[row : row + 32, at : at + 64] = ku1[tap]
+            at = (a * 4 + e + j) * 32
+            wus[row : row + 32, at : at + 32] = ku1[tap][:, :32]
+            wul[row : row + 32, at : at + 32] = ku1[tap][:, 32:]
         at = a * 3 + e
         wu2[f * 64 : f * 64 + 64, at * 128 : at * 128 + 128] = ku2[tap]
 
@@ -226,32 +330,6 @@
     for j in range(2):
         wl0[j * 16 : j * 16 + 16, j * 32 : j * 32 + 32] = lift0[...]
 
-    def selector(target, rule):
-        a = lax.broadcasted_iota(jnp.int32, target.shape, 0)
-        b = lax.broadcasted_iota(jnp.int32, target.shape, 1)
-        target[...] = rule(a, b).astype(F32).astype(BF16)
-
-    def pick_rule(a, b):
-        cell = (b & 127) - 32
-        return (cell >= 0) & (cell < 64) & (a == 2 * cell + (b >> 7))
-
-    def rule2(tall, flat, spread):
-        q, at = tall >> 7, (tall & 127) - 32
-        w = flat & 31
-        return (q == (flat >> 5)) & (at >= 2 * w) & (at < 2 * w + spread)
-
-    def rule3(tall, flat, spread):
-        r, q, at = tall >> 9, (tall >> 7) & 3, (tall & 127) - 32
-        w = flat & 15
-        return (q == (flat >> 5)) & (r == ((flat >> 4) & 1)) & (at >= 4 * w) & (at < 4 * w + spread)
-
-    def rule_edge(tall, flat, spread):
-        q, at, m = tall >> 7, tall & 127, flat & 31
-        size = jnp.where(m < 16, 2, 4)
-        start = jnp.where(m < 16, 2 * m, 4 * m - 32)
-        return (q == (flat >> 5)) & (m < 20) & (at >= start) & (at < start + (size if spread else 1))
-
-    selector(pick, pick_rule)
     selector(grow, lambda a, b: a == (((b & 127) + (b >> 7) + 1) >> 1) + 31)
     selector(fold2, lambda a, b: rule2(a, b, 1))
     selector(unfold2, lambda a, b: rule2(b, a, 2))
@@ -260,75 +338,6 @@
     selector(fold_edge, lambda a, b: rule_edge(a, b, False))
     selector(unfold_edge, lambda a, b: rule_edge(b, a, True))
 
-    def shifted(src, edge, target, base):
-        for dz, dy in PLANE:
-            p0, n0, s0 = region(dz, 8, 1)
-            p1, n1, s1 = region(dy, 16, 1)
-            ok = within(dz, dy)
-            ok_left = (ok * inside_left).astype(F32)
-            ok_right = (ok * inside_right).astype(F32)
-            ok = ok.astype(F32)
-            left_edge = edge[0, dz + 1, dy + 1].astype(F32) * ok_left
-            right_edge = edge[1, dz + 1, dy + 1].astype(F32) * ok_right
-
-            def body(i, _):
-                i0, i1 = lax.div(i, n1), lax.rem(i, n1)
-                r = (s0 + i0) * 16 + s1 + i1
-                row = src[p0 + i0, p1 + i1].astype(F32)
-                if (dz, dy) != (0, 0):
-                    row = row * ok
-                left = pltpu.roll(left_edge, lax.rem(128 - r, 128), 1)
-                right = pltpu.roll(right_edge, 127 - r, 1)
-                d, h = base + p0 + i0, base + p1 + i1
-                target[d, h, 0:16, :] = jnp.where(lane == 0, left, pltpu.roll(row, 1, 1)).astype(BF16)
-                target[d, h, 16:32, :] = row.astype(BF16)
-                target[d, h, 32:48, :] = jnp.where(
-                    lane == 127, right, pltpu.roll(row, 127, 1)
-                ).astype(BF16)
-                return 0
-
-            lax.fori_loop(0, n0 * n1, body, 0, unroll=min(4, n0 * n1))
-
-    wait_recv(rows_in + edges_in)
-    shifted(vol, edge0, stack0, 0)
-
-    def encode(i, _):
-        d, h = lax.div(i, 4) * 2, lax.rem(i, 4) * 4
-        cells = [stack0[pl.ds(d + j, 3), pl.ds(h, 6)].reshape(864, 128) for j in range(2)]
-        total = jnp.dot(wa0[...], jnp.concatenate(cells, axis=1), preferred_element_type=F32)
-        halves = [
-            leaky(total[:, j * 128 : j * 128 + 128] + bias0[...]).astype(BF16) for j in range(2)
-        ]
-        for j in range(2):
-            zero[1 + d + j, pl.ds(1 + h, 4)] = halves[j].reshape(4, 16, 128)
-        top = jnp.maximum(halves[0], halves[1]).reshape(2, 2, 16, 128)
-        top = jnp.maximum(top[:, 0], top[:, 1]).reshape(32, 128)
-        both = jnp.dot(top, pick[...], preferred_element_type=F32)
-        best = jnp.maximum(both[:, :128], both[:, 128:])
-        pool0[3 + lax.div(d, 2), pl.ds(3 + lax.div(h, 2), 2)] = best.astype(BF16).reshape(2, 16, 128)
-        pair0[3 + lax.div(d, 2), 2 + lax.div(h, 4)] = (
-            best[:16] + pltpu.roll(best[16:], 64, 1)
-        ).astype(BF16)
-        return 0
-
-    lax.fori_loop(0, 16, encode, 0, unroll=2)
-
-    def pack1(r, carry):
-        first, last = carry
-        row = pool0[3 + lax.div(r, 8), 3 + lax.rem(r, 8)].astype(F32)
-        mine = lax.div(lane, 4) == r
-        first = jnp.where(mine, pltpu.roll(row, lax.rem(4 * r + 96, 128), 1), first)
-        last = jnp.where(mine, pltpu.roll(row, lax.rem(4 * r + 35, 128), 1), last)
-        return first, last
-
-    blank = jnp.zeros((16, 128), F32)
-    first, last = lax.fori_loop(0, 32, pack1, (blank, blank), unroll=4)
-    mine1[0] = first.astype(BF16)
-    mine1[1] = last.astype(BF16)
-    rows1 = send_rows(pair0, (4, 4), (3, 2))
-    edges1 = send_edges(mine1, edge1, PLANE, 1)
-    sent += rows1 + edges1
-
     wait_recv(rows1 + edges1)
 
     def packz(r, carry):
@@ -338,7 +347,7 @@
         last = jnp.where(lane == r, pltpu.roll(row, lax.rem(r + 1, 128), 1), last)
         return first, last
 
-    first, last = lax.fori_loop(0, 128, packz, (blank, blank), unroll=4)
+    first, last = lax.fori_loop(0, 128, packz, (blank, blank), unroll=8)
     minez[0] = first.astype(BF16)
     minez[1] = last.astype(BF16)
     rowsz = send_rows(zero, (8, 16), (1, 1))
@@ -370,7 +379,7 @@
             pool0[p0 + i0, p1 + i1] = row.astype(BF16)
             return 0
 
-        lax.fori_loop(0, n0 * n1, join_rows, 0, unroll=3 if n0 * n1 == 9 else 4)
+        lax.fori_loop(0, n0 * n1, join_rows, 0, unroll=9 if n0 * n1 == 9 else 6 if n0 * n1 < 32 else 8)
 
     lanes_ok = ((lane >= 32) | (x > 0)) & ((lane < 96) | (x < nx - 1))
     lanes_ok = lanes_ok.astype(jnp.int32)
@@ -402,12 +411,12 @@
             value = leaky(combine(total, 64, 1, j) + bias1[...])
             for g in range(2):
                 row = jnp.where(keeps(d + j - 2, h + g - 2, 4, 8), value[g * 32 : g * 32 + 32], 0.0)
-                join1[d + j, h + g, 0:32, :] = row.astype(BF16)
+                skip1[d + j, h + g] = row.astype(BF16)
                 best = row if best is None else jnp.maximum(best, row)
         pool1[lax.div(d, 2), lax.div(h, 2)] = pairs(best, 1).astype(BF16)
         return 0
 
-    lax.fori_loop(0, 24, second, 0, unroll=2)
+    lax.fori_loop(0, 24, second, 0, unroll=4)
 
 
     def third(h, _):
@@ -415,7 +424,7 @@
         total = jnp.dot(w2[...], jnp.concatenate(cells, axis=1), preferred_element_type=F32)
         for j in range(2):
             value = leaky(combine(total, 64, 2, j) + bias2[...])
-            join2[2 + j, 2 + h, 0:64, :] = jnp.where(own, value, 0.0).astype(BF16)
+            skip2[2 + j, 2 + h] = jnp.where(own, value, 0.0).astype(BF16)
         return 0
 
     lax.fori_loop(0, 4, third, 0, unroll=2)
@@ -424,7 +433,7 @@
     for h in range(2):
         best = None
         for j, g in itertools.product(range(2), repeat=2):
-            row = join2[2 + j, 2 + 2 * h + g, 0:64, :].astype(F32)
+            row = skip2[2 + j, 2 + 2 * h + g].astype(F32)
             best = row if best is None else jnp.maximum(best, row)
             r = j * 4 + 2 * h + g
             here = lax.div(lane, 4) == r
@@ -455,14 +464,35 @@
         if (dz, dy) != (0, 0)
     ]
     for j, g in itertools.product(range(2), repeat=2):
-        rows = [join2[2 + j, 2 + 2 * g + p, 0:64, :] for p in range(2)]
+        rows = [skip2[2 + j, 2 + 2 * g + p] for p in range(2)]
         folded2[2 + j, 1 + g] = fold(rows, 2, fold2)
     rows2 = send_rows(folded2, (2, 2), (2, 1))
     sent += pools2 + rows2
     sent += edges2
 
+    def upper_one_skip(i, _):
+        d, h = lax.div(i, 5) * 2, lax.rem(i, 5) * 2
+        cells = [skip1[pl.ds(d + j, 3), pl.ds(h, 4)].reshape(384, 128) for j in range(2)]
+        total = jnp.dot(wus[...], jnp.concatenate(cells, axis=1), preferred_element_type=F32)
+        for j in range(2):
+            part1[i, j] = combine(total, 64, 1, j) + off1[...]
+        return 0
+
+    lax.fori_loop(0, 15, upper_one_skip, 0, unroll=3)
+
     wait_recv(rowsz + edgesz)
-    shifted(zero, edgez, join0, 1)
+    shifted(zero, edgez, stack0)
+
+    def decode_skip(i, _):
+        d, h = lax.div(i, 4) * 2, lax.rem(i, 4) * 4
+        cells = [stack0[pl.ds(d + j, 3), pl.ds(h, 6)].reshape(864, 128) for j in range(2)]
+        total = jnp.dot(wds[...], jnp.concatenate(cells, axis=1), preferred_element_type=F32)
+        for j in range(2):
+            value = total[:, j * 128 : j * 128 + 128] + off0[...]
+            part0[d + j, pl.ds(h, 4)] = value.reshape(4, 16, 128)
+        return 0
+
+    lax.fori_loop(0, 16, decode_skip, 0, unroll=4)
 
     wait_recv(edges2 + pools2)
     for side in range(2):
@@ -503,17 +533,22 @@
         d, h = lax.div(i, 2), lax.rem(i, 2) * 2
         cells = [pool2[pl.ds(d, 3), pl.ds(h + j, 3)].reshape(576, 128) for j in range(2)]
         total = jnp.dot(w3[...], jnp.concatenate(cells, axis=1), preferred_element_type=F32)
-        low = []
         for j in range(2):
             value = leaky(combine(total, 128, 4, j) + bias3[...])
-            low.append(jnp.where(keeps(d - 1, h + j - 1, 1, 2), value, 0.0).astype(BF16))
-        up = jnp.dot(lift2[...], jnp.concatenate(low, axis=1), preferred_element_type=F32).astype(BF16)
-        for j in range(2):
-            for p, q in itertools.product(range(2), repeat=2):
-                join2[2 * d + p, 2 * (h + j) + q, 64:128, :] = up[:, j * 128 : j * 128 + 128]
-        return 0
-
-    lax.fori_loop(0, 6, coarsest, 0, unroll=3)
+            row = jnp.where(keeps(d - 1, h + j - 1, 1, 2), value, 0.0)
+            low3[d, h + j] = row.astype(BF16)
+        return 0
+
+    def lifts(matrix, rows):
+        wide = jnp.dot(
+            matrix[...], jnp.concatenate(rows, axis=1), preferred_element_type=F32
+        ).astype(BF16)
+        return [wide[:, k * 128 : k * 128 + 128] for k in range(len(rows))]
+
+    lax.fori_loop(0, 6, coarsest, 0, unroll=6)
+    for d in range(3):
+        for h, row in enumerate(lifts(lift2, [low3[d, h] for h in range(4)])):
+            up2[d, h] = row
 
     wait_recv(rows2)
     for d in range(6):
@@ -525,7 +560,7 @@
         for k, g in enumerate((0, 3) if near else range(4)):
             for q, p in itertools.product(range(2), repeat=2):
                 at = (q * 2 + p) * 128
-                join2[d, 2 * g + p, q * 32 : q * 32 + 32, :] = parts[
+                skip2[d, 2 * g + p, q * 32 : q * 32 + 32, :] = parts[
                     k * 32 : k * 32 + 32, at : at + 128
                 ]
     for dz, dy in PLANE:
@@ -537,65 +572,84 @@
         keep = ok.astype(F32)
         for i0, i1 in itertools.product(range(n0), range(n1)):
             r = (s0 + i0) * 4 + s1 + i1
-            row = join2[p0 + i0, p1 + i1, 0:64, :].astype(F32) * keep
+            row = skip2[p0 + i0, p1 + i1].astype(F32) * keep
             left = pltpu.roll(left_edge, (28 - 4 * r) % 128, 1)
             right = pltpu.roll(right_edge, (96 - 4 * r) % 128, 1)
             row = jnp.where((lane >= 28) & (lane < 32), left, row)
             row = jnp.where((lane >= 96) & (lane < 100), right, row)
-            join2[p0 + i0, p1 + i1, 0:64, :] = row.astype(BF16)
+            skip2[p0 + i0, p1 + i1] = row.astype(BF16)
 
     def upper_two(i, _):
         d, h = lax.div(i, 6) * 2, lax.rem(i, 6)
-        cells = [join2[pl.ds(d + j, 3), pl.ds(h, 3)].reshape(1152, 128) for j in range(2)]
+        cells = []
+        for j in range(2):
+            pieces = []
+            for a, e in itertools.product(range(3), repeat=2):
+                pieces.append(skip2[d + j + a, h + e])
+                pieces.append(up2[lax.div(i, 6) + (j + a) // 2, lax.div(h + e, 2)])
+            cells.append(jnp.concatenate(pieces, axis=0))
         total = jnp.dot(wu2[...], jnp.concatenate(cells, axis=1), preferred_element_type=F32)
-        low = []
         for j in range(2):
             value = leaky(combine(total, 64, 2, j) + off2[...])
-            low.append(jnp.where(keeps(d + j - 1, h - 1, 2, 4), value, 0.0).astype(BF16))
-        up = jnp.dot(lift1[...], jnp.concatenate(low, axis=1), preferred_element_type=F32).astype(BF16)
-        for j in range(2):
-            for p, q in itertools.product(range(2), repeat=2):
-                join1[2 * (d + j) + p, 2 * h + q, 32:64, :] = up[:, j * 128 : j * 128 + 128]
+            low2[d + j, h] = jnp.where(keeps(d + j - 1, h - 1, 2, 4), value, 0.0).astype(BF16)
         return 0
 
     lax.fori_loop(0, 12, upper_two, 0, unroll=3)
+    for d in range(4):
+        for h, row in enumerate(lifts(lift1, [low2[d, h] for h in range(6)])):
+            lifted1[d, h] = row
 
     def upper_one(i, _):
         d, h = lax.div(i, 5) * 2, lax.rem(i, 5) * 2
-        cells = [join1[pl.ds(d + j, 3), pl.ds(h, 4)].reshape(768, 128) for j in range(2)]
-        total = jnp.dot(wu1[...], jnp.concatenate(cells, axis=1), preferred_element_type=F32)
-        low = []
-        for j in range(2):
-            value = leaky(combine(total, 64, 1, j) + off1[...])
+        cells = []
+        for j in range(2):
+            pieces = [
+                lifted1[lax.div(i, 5) + (j + a) // 2, lax.rem(i, 5) + g // 2]
+                for a, g in itertools.product(range(3), range(4))
+            ]
+            cells.append(jnp.concatenate(pieces, axis=0))
+        total = jnp.dot(wul[...], jnp.concatenate(cells, axis=1), preferred_element_type=F32)
+        for j in range(2):
+            value = leaky(combine(total, 64, 1, j) + part1[i, j])
             kept = [
                 jnp.where(keeps(d + j - 1, h + g - 1, 4, 8), value[g * 32 : g * 32 + 32], 0.0)
                 for g in range(2)
             ]
-            low.append(jnp.concatenate(kept, axis=0).astype(BF16))
-        up = jnp.dot(wl0[...], jnp.concatenate(low, axis=1), preferred_element_type=F32).astype(BF16)
-        up = jnp.concatenate([up[:, :128], up[:, 128:]], axis=0)
-        wide = jnp.dot(up, grow[...], preferred_element_type=F32).astype(BF16)
-        for j, g in itertools.product(range(2), repeat=2):
-            at = (j * 2 + g) * 16
-            three = [wide[at : at + 16, f * 128 : f * 128 + 128] for f in range(3)]
-            three = jnp.concatenate(three, axis=0)
-            for p, q in itertools.product(range(2), repeat=2):
-                join0[2 * (d + j) + p, 2 * (h + g) + q, 48:96, :] = three
-        return 0
-
-    lax.fori_loop(0, 15, upper_one, 0, unroll=3)
+            low1[i, j] = jnp.concatenate(kept, axis=0).astype(BF16)
+        return 0
+
+    lax.fori_loop(0, 15, upper_one, 0, unroll=5)
+    for d in range(3):
+        order = list(itertools.product(range(2), range(5)))
+        rows = lifts(wl0, [low1[d * 5 + h, j] for j, h in order])
+        wide = jnp.dot(
+            jnp.concatenate(rows, axis=0), grow[...], preferred_element_type=F32
+        ).astype(BF16)
+        for k, (j, h) in enumerate(order):
+            for g, f in itertools.product(range(2), range(3)):
+                at = k * 32 + g * 16
+                lifted0[2 * d + j, 2 * h + g, f * 16 : f * 16 + 16, :] = wide[
+                    at : at + 16, f * 128 : f * 128 + 128
+                ]
 
     def decode(i, _):
         d, h = lax.div(i, 4) * 2, lax.rem(i, 4) * 4
-        cells = [join0[pl.ds(d + 1 + j, 3), pl.ds(h + 1, 6)].reshape(1728, 128) for j in range(2)]
-        total = jnp.dot(wd0[...], jnp.concatenate(cells, axis=1), preferred_element_type=F32)
-        for j in range(2):
-            value = leaky(total[:, j * 128 : j * 128 + 128] + off0[...])
+        cells = []
+        for j in range(2):
+            pieces = [
+                lifted0[lax.div(d, 2) + (1 + j + a) // 2, lax.div(h, 2) + (1 + g) // 2]
+                for a, g in itertools.product(range(3), range(6))
+            ]
+            cells.append(jnp.concatenate(pieces, axis=0))
+        total = jnp.dot(wdl[...], jnp.concatenate(cells, axis=1), preferred_element_type=F32)
+        for j in range(2):
+            held = part0[d + j, pl.ds(h, 4)].reshape(64, 128)
+            value = leaky(total[:, j * 128 : j * 128 + 128] + held)
             for g in range(4):
                 xf[pl.ds((d + j) * 16 + h + g, 16, stride=128), :] = value[g * 16 : g * 16 + 16]
         return 0
 
-    lax.fori_loop(0, 16, decode, 0, unroll=2)
+    lax.fori_loop(0, 16, decode, 0, unroll=4)
     for c in range(16):
         out_ref[c] = xf[pl.ds(c * 128, 128), :].astype(BF16).reshape(8, 16, 128)
 
@@ -641,12 +695,14 @@
     scratch = [
         wide(2048), tile(10, 18, 16, 128), tile(2, 3, 3, 16, 128), tile(2, 16, 128), tile(10, 18, 48, 128),
         tile(10, 18, 16, 128), tile(2, 3, 3, 16, 128), tile(2, 16, 128),
-        tile(10, 14, 16, 128), tile(10, 8, 16, 128), tile(2, 3, 3, 16, 128), tile(2, 16, 128),
-        tile(8, 12, 64, 128), tile(4, 6, 32, 128), tile(6, 8, 128, 128),
+        tile(4, 8, 16, 128), tile(10, 14, 16, 128), tile(10, 8, 16, 128), tile(2, 3, 3, 16, 128), tile(2, 16, 128),
+        tile(8, 12, 32, 128), tile(4, 6, 64, 128), tile(4, 6, 32, 128), tile(4, 6, 32, 128),
+        tile(6, 8, 64, 128), tile(3, 4, 128, 128), tile(3, 4, 64, 128),
         tile(5, 6, 64, 128), tile(2, 5, 3, 64, 128), tile(2, 5, 3, 16, 128), tile(2, 16, 128),
-        tile(6, 4, 32, 128), tile(5, 3, 16, 128), tile(12, 20, 96, 128),
-        tile(64, 864), tile(64, 1728), tile(192, 192), tile(192, 288), tile(384, 576),
-        tile(192, 1152), tile(192, 768), tile(32, 64),
+        tile(6, 4, 32, 128), tile(5, 3, 16, 128), tile(15, 2, 64, 128), tile(6, 10, 48, 128),
+        pltpu.VMEM((8, 16, 16, 128), F32), pltpu.VMEM((15, 2, 64, 128), F32),
+        tile(64, 864), tile(64, 864), tile(64, 864), tile(192, 192), tile(192, 288), tile(384, 576),
+        tile(192, 1152), tile(192, 384), tile(192, 384), tile(32, 64),
         tile(128, 256), tile(128, 384),
         tile(512, 128), tile(128, 512), tile(1024, 128), tile(128, 1024), tile(512, 128), tile(128, 512),
         wide(64), wide(64), wide(64), wide(128), wide(64), wide(64), wide(64),

time: 81.5 us -> 62.8 us (0.77)
  Pallas kernels: 79.5 us -> 60.8 us
    pallas_call x1, Pallas kernels: 79.5 us -> 60.8 us  [per_device(): pl.pallas_call(kernel, out_shape=jax.ShapeDtypeStruct(volume.shape, BF16)...]
where the time goes in v3:
time: 62.8 us; the launch traced here: 62.7 us
  Pallas kernels  60.8 us (97%)
  local copies, waits for them, and re-layouts  1.89 us (3%)
    pallas_call x1, Pallas kernels, per_device(): pl.pallas_call(kernel, out_shape=jax.ShapeDtypeStruct(volume.shape, BF16)...  60.8 us
    unnamed x1, local copies, waits for them, and re-layouts  1.89 us

profile of v3, /device:TPU:1, one launch (start us, length us, event | category | flops | bytes accessed | tf_op | source)
XLA Modules:
  0.0 62.7 jit_solution(13539580768956589416)
XLA Ops:
  0.0 60.8 %shard_map.172 = bf16[16,8,16,128]{3,2,1,0:T(8,128)(2,1)} custom-call(bf16[16,8,16,128]{3,2,1,0:T(8,128)(2,1)} %refs_0_.1, bf16[27,16,16]{2,1,0:T(8,128)(2,1)} %bitcast.32, f32[1,16]{1,0:T(1,128)} %bitcast.35, bf16[27,16,32]{2,1,0:T(8,128)(2,1)} %bitcast.33, f32[1,32]{1,0:T(1,128)} %bitcast.36, bf16[27,32,64]{2,1,0:T(8,128)(2,1)} %bitcast.30, ...), custom_call_target="tpu_custom_call" | custom-call | tf_op jit(solution)/shard_map/pallas_call | solution.py:725
  60.8 1.9 %copy.20 = bf16[16,8,16,128]{3,2,1,0:T(8,128)(2,1)} copy(bf16[16,8,16,128]{3,2,1,0:T(8,128)(2,1)} %shard_map.172) | data formatting | bytes 1048576

commit v4 on v3

--- a/solution.py
+++ b/solution.py
@@ -66,19 +66,18 @@
     def device(dz, dy, dx):
         return (lax.rem(z + dz + nz, nz), lax.rem(y + dy + ny, ny), lax.rem(x + dx + nx, nx))
 
-    beyond = [step for step in FAR if step not in PLANE]
-    others = [(*step, dx) for step in PLANE + beyond for dx in STEPS if (*step, dx) != (0, 0, 0)]
+    others = [(*step, dx) for step in PLANE for dx in STEPS if (*step, dx) != (0, 0, 0)]
+    loads = [
+        pltpu.make_async_copy(source, local, load_sem.at[k])
+        for k, (source, local) in enumerate(zip(sources, locals_))
+    ]
+    loads[0].start()
     barrier = pltpu.get_barrier_semaphore()
     for step in others:
         pl.semaphore_signal(
             barrier, inc=1, device_id=device(*step), device_id_type=pl.DeviceIdType.MESH
         )
-
-    loads = [
-        pltpu.make_async_copy(source, local, load_sem.at[k])
-        for k, (source, local) in enumerate(zip(sources, locals_))
-    ]
-    for load in loads:
+    for load in loads[1:]:
         load.start()
 
     count = itertools.count()
@@ -132,6 +131,11 @@
     inside_left = (x > 0).astype(jnp.int32)
     inside_right = (x < nx - 1).astype(jnp.int32)
 
+    def only(keep, values):
+        if keep.dtype != jnp.bool_:
+            keep = (lane * 0 + keep) > 0
+        return jnp.where(keep, values, jnp.zeros((), values.dtype))
+
     def within(dz, dy):
         pz, py = z + dz, y + dy
         ok = (pz >= 0) & (pz < nz) & (py >= 0) & (py < ny)
@@ -159,9 +163,10 @@
 
     pl.semaphore_wait(barrier, len(others))
     sent = []
+    near_in = send_edges(mine0, edge0, [(0, 0)], 1)
     rows_in = send_rows(vol, (8, 16), (1, 1))
-    edges_in = send_edges(mine0, edge0, PLANE, 1)
-    sent += rows_in + edges_in
+    edges_in = send_edges(mine0, edge0, RING, 1)
+    sent += near_in + rows_in + edges_in
 
     for load in loads[1:]:
         load.wait()
@@ -218,37 +223,60 @@
         return (q == (flat >> 5)) & (m < 20) & (at >= start) & (at < start + (size if spread else 1))
 
     selector(pick, pick_rule)
-    def shifted(src, edge, target):
-        for dz, dy in PLANE:
+    def shifted(src, edge, target, steps):
+        for dz, dy in steps:
             p0, n0, s0 = region(dz, 8, 1)
             p1, n1, s1 = region(dy, 16, 1)
             ok = within(dz, dy)
-            ok_left = (ok * inside_left).astype(F32)
-            ok_right = (ok * inside_right).astype(F32)
-            ok = ok.astype(F32)
-            left_edge = edge[0, dz + 1, dy + 1].astype(F32) * ok_left
-            right_edge = edge[1, dz + 1, dy + 1].astype(F32) * ok_right
+            left_edge = only(ok * inside_left, edge[0, dz + 1, dy + 1])
+            right_edge = only(ok * inside_right, edge[1, dz + 1, dy + 1])
 
             def body(i, _):
                 i0, i1 = lax.div(i, n1), lax.rem(i, n1)
                 r = (s0 + i0) * 16 + s1 + i1
-                row = src[p0 + i0, p1 + i1].astype(F32)
-                if (dz, dy) != (0, 0):
-                    row = row * ok
+                row = only(ok, src[p0 + i0, p1 + i1])
                 left = pltpu.roll(left_edge, lax.rem(128 - r, 128), 1)
                 right = pltpu.roll(right_edge, 127 - r, 1)
                 d, h = p0 + i0, p1 + i1
-                target[d, h, 0:16, :] = jnp.where(lane == 0, left, pltpu.roll(row, 1, 1)).astype(BF16)
-                target[d, h, 16:32, :] = row.astype(BF16)
+                target[d, h, 0:16, :] = jnp.where(lane == 0, left, pltpu.roll(row, 1, 1))
+                target[d, h, 16:32, :] = row
                 target[d, h, 32:48, :] = jnp.where(
                     lane == 127, right, pltpu.roll(row, 127, 1)
-                ).astype(BF16)
+                )
                 return 0
 
             lax.fori_loop(0, n0 * n1, body, 0, unroll=min(8, n0 * n1))
 
+    def shift_own(src, target):
+        def spread(i, _):
+            d, h = 1 + lax.div(i, 16), 1 + lax.rem(i, 16)
+            row = src[d, h]
+            target[d, h, 0:16, :] = pltpu.roll(row, 1, 1)
+            target[d, h, 16:32, :] = row
+            target[d, h, 32:48, :] = pltpu.roll(row, 127, 1)
+            return 0
+
+        lax.fori_loop(0, 128, spread, 0, unroll=8)
+
+    def close_own(edge, target):
+        left_edge = only(inside_left, edge[0, 1, 1])
+        right_edge = only(inside_right, edge[1, 1, 1])
+
+        def close(r, _):
+            d, h = 1 + lax.div(r, 16), 1 + lax.rem(r, 16)
+            left = pltpu.roll(left_edge, lax.rem(128 - r, 128), 1)
+            right = pltpu.roll(right_edge, 127 - r, 1)
+            target[d, h, 0:16, :] = jnp.where(lane == 0, left, target[d, h, 0:16, :])
+            target[d, h, 32:48, :] = jnp.where(lane == 127, right, target[d, h, 32:48, :])
+            return 0
+
+        lax.fori_loop(0, 128, close, 0, unroll=8)
+
+    shift_own(vol, stack0)
+    wait_recv(near_in)
+    close_own(edge0, stack0)
     wait_recv(rows_in + edges_in)
-    shifted(vol, edge0, stack0)
+    shifted(vol, edge0, stack0, RING)
 
     def encode(i, _):
         d, h = lax.div(i, 4) * 2, lax.rem(i, 4) * 4
@@ -275,19 +303,22 @@
 
     def pack1(r, carry):
         first, last = carry
-        row = pool0[3 + lax.div(r, 8), 3 + lax.rem(r, 8)].astype(F32)
+        row = pool0[3 + lax.div(r, 8), 3 + lax.rem(r, 8)]
         mine = lax.div(lane, 4) == r
         first = jnp.where(mine, pltpu.roll(row, lax.rem(4 * r + 96, 128), 1), first)
         last = jnp.where(mine, pltpu.roll(row, lax.rem(4 * r + 35, 128), 1), last)
         return first, last
 
-    blank = jnp.zeros((16, 128), F32)
+    blank = jnp.zeros((16, 128), BF16)
     first, last = lax.fori_loop(0, 32, pack1, (blank, blank), unroll=8)
-    mine1[0] = first.astype(BF16)
-    mine1[1] = last.astype(BF16)
+    mine1[0] = first
+    mine1[1] = last
+    near1 = send_edges(mine1, edge1, [(0, 0)], 1)
     rows1 = send_rows(pair0, (4, 4), (3, 2))
-    edges1 = send_edges(mine1, edge1, PLANE, 1)
-    sent += rows1 + edges1
+    edges1 = send_edges(mine1, edge1, RING, 1)
+    sent += near1 + rows1 + edges1
+
+    own = (lane >= 32) & (lane < 96)
 
     for ref in (wds, wdl, wus, wul, wl0):
         ref[...] = jnp.zeros(ref.shape, BF16)
@@ -338,48 +369,52 @@
     selector(fold_edge, lambda a, b: rule_edge(a, b, False))
     selector(unfold_edge, lambda a, b: rule_edge(b, a, True))
 
-    wait_recv(rows1 + edges1)
-
     def packz(r, carry):
         first, last = carry
-        row = zero[1 + lax.div(r, 16), 1 + lax.rem(r, 16)].astype(F32)
+        row = zero[1 + lax.div(r, 16), 1 + lax.rem(r, 16)]
         first = jnp.where(lane == r, pltpu.roll(row, r, 1), first)
         last = jnp.where(lane == r, pltpu.roll(row, lax.rem(r + 1, 128), 1), last)
         return first, last
 
     first, last = lax.fori_loop(0, 128, packz, (blank, blank), unroll=8)
-    minez[0] = first.astype(BF16)
-    minez[1] = last.astype(BF16)
+    minez[0] = first
+    minez[1] = last
+    def join_regions(steps):
+        for dz, dy in steps:
+            p0, n0, s0 = region(dz, 4, 3)
+            p1, n1, s1 = region(dy, 8, 3)
+            ok = within(dz, dy)
+            left_edge = only(ok * inside_left, edge1[0, dz + 1, dy + 1])
+            right_edge = only(ok * inside_right, edge1[1, dz + 1, dy + 1])
+            keep = (own.astype(jnp.int32) * ok) > 0
+
+            def join_rows(i, _):
+                i0, i1 = lax.div(i, n1), lax.rem(i, n1)
+                r = (s0 + i0) * 8 + s1 + i1
+                if (dz, dy) == (0, 0):
+                    row = pool0[p0 + i0, p1 + i1]
+                else:
+                    at = p1 + i1 + 1
+                    row = pair0[p0 + i0, lax.div(at, 2)]
+                    row = only(keep, pltpu.roll(row, 64 * lax.rem(at, 2), 1))
+                left = pltpu.roll(left_edge, lax.rem(157 - 4 * r, 128), 1)
+                right = pltpu.roll(right_edge, lax.rem(224 - 4 * r, 128), 1)
+                row = jnp.where((lane >= 29) & (lane < 32), left, row)
+                row = jnp.where((lane >= 96) & (lane < 99), right, row)
+                pool0[p0 + i0, p1 + i1] = row
+                return 0
+
+            lax.fori_loop(0, n0 * n1, join_rows, 0, unroll=9 if n0 * n1 == 9 else 6 if n0 * n1 < 32 else 8)
+
+    shift_own(zero, stack0)
+    wait_recv(near1)
+    join_regions([(0, 0)])
+    wait_recv(rows1 + edges1)
+
     rowsz = send_rows(zero, (8, 16), (1, 1))
     edgesz = send_edges(minez, edgez, PLANE, 1)
     sent += rowsz + edgesz
-
-    own = (lane >= 32) & (lane < 96)
-    for dz, dy in PLANE:
-        p0, n0, s0 = region(dz, 4, 3)
-        p1, n1, s1 = region(dy, 8, 3)
-        ok = within(dz, dy)
-        left_edge = edge1[0, dz + 1, dy + 1].astype(F32) * (ok * inside_left).astype(F32)
-        right_edge = edge1[1, dz + 1, dy + 1].astype(F32) * (ok * inside_right).astype(F32)
-        keep = ok.astype(F32)
-
-        def join_rows(i, _):
-            i0, i1 = lax.div(i, n1), lax.rem(i, n1)
-            r = (s0 + i0) * 8 + s1 + i1
-            if (dz, dy) == (0, 0):
-                row = pool0[p0 + i0, p1 + i1].astype(F32)
-            else:
-                at = p1 + i1 + 1
-                row = pair0[p0 + i0, lax.div(at, 2)].astype(F32) * keep
-                row = jnp.where(own, pltpu.roll(row, 64 * lax.rem(at, 2), 1), 0.0)
-            left = pltpu.roll(left_edge, lax.rem(157 - 4 * r, 128), 1)
-            right = pltpu.roll(right_edge, lax.rem(224 - 4 * r, 128), 1)
-            row = jnp.where((lane >= 29) & (lane < 32), left, row)
-            row = jnp.where((lane >= 96) & (lane < 99), right, row)
-            pool0[p0 + i0, p1 + i1] = row.astype(BF16)
-            return 0
-
-        lax.fori_loop(0, n0 * n1, join_rows, 0, unroll=9 if n0 * n1 == 9 else 6 if n0 * n1 < 32 else 8)
+    join_regions(RING)
 
     lanes_ok = ((lane >= 32) | (x > 0)) & ((lane < 96) | (x < nx - 1))
     lanes_ok = lanes_ok.astype(jnp.int32)
@@ -416,7 +451,7 @@
         pool1[lax.div(d, 2), lax.div(h, 2)] = pairs(best, 1).astype(BF16)
         return 0
 
-    lax.fori_loop(0, 24, second, 0, unroll=4)
+    lax.fori_loop(0, 24, second, 0, unroll=8)
 
 
     def third(h, _):
@@ -427,20 +462,20 @@
             skip2[2 + j, 2 + h] = jnp.where(own, value, 0.0).astype(BF16)
         return 0
 
-    lax.fori_loop(0, 4, third, 0, unroll=2)
-    first = jnp.zeros((64, 128), F32)
-    last = jnp.zeros((64, 128), F32)
+    lax.fori_loop(0, 4, third, 0, unroll=4)
+    first = jnp.zeros((64, 128), BF16)
+    last = jnp.zeros((64, 128), BF16)
     for h in range(2):
         best = None
         for j, g in itertools.product(range(2), repeat=2):
-            row = skip2[2 + j, 2 + 2 * h + g].astype(F32)
+            row = skip2[2 + j, 2 + 2 * h + g]
             best = row if best is None else jnp.maximum(best, row)
             r = j * 4 + 2 * h + g
             here = lax.div(lane, 4) == r
             first = jnp.where(here, pltpu.roll(row, (4 * r + 96) % 128, 1), first)
             last = jnp.where(here, pltpu.roll(row, (4 * r + 36) % 128, 1), last)
         best = pairs(best, 2)
-        pool2[2, 2 + h] = best.astype(BF16)
+        pool2[2, 2 + h] = best
         here = lax.div(lane, 8) == 4 + h
         first = jnp.where(here, pltpu.roll(best, 8 * h, 1), first)
         last = jnp.where(here, pltpu.roll(best, 8 * h + 72, 1), last)
@@ -451,8 +486,8 @@
             jnp.concatenate(pieces, axis=1), matrix[...], preferred_element_type=F32
         ).astype(BF16)
 
-    mine2[0] = fold([first.astype(BF16)], 4, fold_edge)
-    mine2[1] = fold([last.astype(BF16)], 4, fold_edge)
+    mine2[0] = fold([first], 4, fold_edge)
+    mine2[1] = fold([last], 4, fold_edge)
     pieces = [pool2[2, 2 + r][q * 16 : q * 16 + 16] for r in range(2) for q in range(4)]
     folded3[2, 1] = jnp.dot(
         jnp.concatenate(pieces, axis=1), fold3[...], preferred_element_type=F32
@@ -481,7 +516,8 @@
     lax.fori_loop(0, 15, upper_one_skip, 0, unroll=3)
 
     wait_recv(rowsz + edgesz)
-    shifted(zero, edgez, stack0)
+    close_own(edgez, stack0)
+    shifted(zero, edgez, stack0, RING)
 
     def decode_skip(i, _):
         d, h = lax.div(i, 4) * 2, lax.rem(i, 4) * 4
@@ -518,16 +554,15 @@
                 ]
     for dz, dy in FAR:
         ok = within(dz, dy)
-        left_edge = wide2[0, dz + 2, dy + 1].astype(F32) * (ok * inside_left).astype(F32)
-        right_edge = wide2[1, dz + 2, dy + 1].astype(F32) * (ok * inside_right).astype(F32)
-        keep = ok.astype(F32)
+        left_edge = only(ok * inside_left, wide2[0, dz + 2, dy + 1])
+        right_edge = only(ok * inside_right, wide2[1, dz + 2, dy + 1])
         for r in range(2):
-            row = pool2[2 + dz, 2 + 2 * dy + r].astype(F32) * keep
+            row = only(ok, pool2[2 + dz, 2 + 2 * dy + r])
             left = pltpu.roll(left_edge, (24 - 32 - 8 * r) % 128, 1)
             right = pltpu.roll(right_edge, (96 - 32 - 8 * r) % 128, 1)
             row = jnp.where((lane >= 24) & (lane < 32), left, row)
             row = jnp.where((lane >= 96) & (lane < 104), right, row)
-            pool2[2 + dz, 2 + 2 * dy + r] = row.astype(BF16)
+            pool2[2 + dz, 2 + 2 * dy + r] = row
 
     def coarsest(i, _):
         d, h = lax.div(i, 2), lax.rem(i, 2) * 2
@@ -567,17 +602,16 @@
         p0, n0, s0 = region(dz, 2, 2)
         p1, n1, s1 = region(dy, 4, 2)
         ok = within(dz, dy)
-        left_edge = wide2[0, dz + 2, dy + 1].astype(F32) * (ok * inside_left).astype(F32)
-        right_edge = wide2[1, dz + 2, dy + 1].astype(F32) * (ok * inside_right).astype(F32)
-        keep = ok.astype(F32)
+        left_edge = only(ok * inside_left, wide2[0, dz + 2, dy + 1])
+        right_edge = only(ok * inside_right, wide2[1, dz + 2, dy + 1])
         for i0, i1 in itertools.product(range(n0), range(n1)):
             r = (s0 + i0) * 4 + s1 + i1
-            row = skip2[p0 + i0, p1 + i1].astype(F32) * keep
+            row = only(ok, skip2[p0 + i0, p1 + i1])
             left = pltpu.roll(left_edge, (28 - 4 * r) % 128, 1)
             right = pltpu.roll(right_edge, (96 - 4 * r) % 128, 1)
             row = jnp.where((lane >= 28) & (lane < 32), left, row)
             row = jnp.where((lane >= 96) & (lane < 100), right, row)
-            skip2[p0 + i0, p1 + i1] = row.astype(BF16)
+            skip2[p0 + i0, p1 + i1] = row
 
     def upper_two(i, _):
         d, h = lax.div(i, 6) * 2, lax.rem(i, 6)
@@ -632,26 +666,29 @@
                     at : at + 16, f * 128 : f * 128 + 128
                 ]
 
-    def decode(i, _):
-        d, h = lax.div(i, 4) * 2, lax.rem(i, 4) * 4
-        cells = []
-        for j in range(2):
-            pieces = [
-                lifted0[lax.div(d, 2) + (1 + j + a) // 2, lax.div(h, 2) + (1 + g) // 2]
-                for a, g in itertools.product(range(3), range(6))
-            ]
-            cells.append(jnp.concatenate(pieces, axis=0))
-        total = jnp.dot(wdl[...], jnp.concatenate(cells, axis=1), preferred_element_type=F32)
-        for j in range(2):
-            held = part0[d + j, pl.ds(h, 4)].reshape(64, 128)
-            value = leaky(total[:, j * 128 : j * 128 + 128] + held)
-            for g in range(4):
-                xf[pl.ds((d + j) * 16 + h + g, 16, stride=128), :] = value[g * 16 : g * 16 + 16]
-        return 0
-
-    lax.fori_loop(0, 16, decode, 0, unroll=4)
-    for c in range(16):
-        out_ref[c] = xf[pl.ds(c * 128, 128), :].astype(BF16).reshape(8, 16, 128)
+    def decode(p, _):
+        d = 2 * p
+        for h in range(0, 16, 4):
+            cells = []
+            for j in range(2):
+                pieces = [
+                    lifted0[p + (1 + j + a) // 2, h // 2 + (1 + g) // 2]
+                    for a, g in itertools.product(range(3), range(6))
+                ]
+                cells.append(jnp.concatenate(pieces, axis=0))
+            total = jnp.dot(wdl[...], jnp.concatenate(cells, axis=1), preferred_element_type=F32)
+            for j in range(2):
+                held = part0[d + j, pl.ds(h, 4)].reshape(64, 128)
+                value = leaky(total[:, j * 128 : j * 128 + 128] + held)
+                for g in range(4):
+                    at = (d + j) * 16 + h + g
+                    xf[pl.ds(at, 16, stride=128), :] = value[g * 16 : g * 16 + 16]
+        for c in range(16):
+            rows = xf[pl.ds(pl.multiple_of(c * 128 + p * 32, 32), 32), :].astype(BF16)
+            out_ref[c, pl.ds(d, 2)] = rows.reshape(2, 16, 128)
+        return 0
+
+    lax.fori_loop(0, 4, decode, 0)
 
     wait_send(sent)
 
@@ -724,7 +761,7 @@
     )
     return pl.pallas_call(
         kernel,
-        out_shape=jax.ShapeDtypeStruct(volume.shape, BF16),
+        out_shape=pltpu.VMEM(volume.shape, BF16),
         in_specs=[pl.BlockSpec(memory_space=pltpu.HBM)] * len(operands),
         out_specs=pl.BlockSpec(memory_space=pltpu.VMEM),
         scratch_shapes=[pltpu.VMEM(value.shape, value.dtype) for value in operands] + scratch,

time: 62.8 us -> 54.5 us (0.87)
  Pallas kernels: 60.8 us -> 53.6 us
  local copies, waits for them, and re-layouts: 1.89 us -> 0.8 us
    pallas_call x1, Pallas kernels: 60.8 us -> 53.6 us  [per_device(): pl.pallas_call(kernel, out_shape=pltpu.VMEM(volume.shape, BF16), in_specs...]
    unnamed x1, local copies, waits for them, and re-layouts: 1.89 us -> 0.8 us
where the time goes in v4:
time: 54.5 us; the launch traced here: 54.4 us
  Pallas kernels  53.6 us (98%)
  local copies, waits for them, and re-layouts  0.8 us (1%)
    pallas_call x1, Pallas kernels, per_device(): pl.pallas_call(kernel, out_shape=pltpu.VMEM(volume.shape, BF16), in_specs...  53.6 us

profile of v4, /device:TPU:1, one launch (start us, length us, event | category | flops | bytes accessed | tf_op | source)
XLA Modules:
  0.0 54.4 jit_solution(13068537703037023266)
XLA Ops:
  0.0 53.6 %shard_map.172 = bf16[16,8,16,128]{3,2,1,0:T(8,128)(2,1)S(1)} custom-call(bf16[16,8,16,128]{3,2,1,0:T(8,128)(2,1)} %refs_0_.1, bf16[27,16,16]{2,1,0:T(8,128)(2,1)} %bitcast.32, f32[1,16]{1,0:T(1,128)} %bitcast.35, bf16[27,16,32]{2,1,0:T(8,128)(2,1)} %bitcast.33, f32[1,32]{1,0:T(1,128)} %bitcast.36, bf16[27,32,64]{2,1,0:T(8,128)(2,1)} %bitcast.30, ...), custom_call_target="tpu_custom_call" | custom-call | tf_op jit(solution)/shard_map/pallas_call | solution.py:762
  53.6 0.8 %copy.20 = bf16[16,8,16,128]{3,2,1,0:T(8,128)(2,1)} copy(bf16[16,8,16,128]{3,2,1,0:T(8,128)(2,1)S(1)} %shard_map.172) | data formatting | bytes 1048576

commit v5 on v4

--- a/solution.py
+++ b/solution.py
@@ -149,7 +149,7 @@
         vol[1 + lax.div(r, 16), 1 + lax.rem(r, 16)] = xf[pl.ds(r, 16, stride=128), :].astype(BF16)
         return 0
 
-    lax.fori_loop(0, 128, to_row, 0, unroll=8)
+    lax.fori_loop(0, 128, to_row, 0, unroll=16)
     row_id = lax.broadcasted_iota(jnp.int32, (32, 2048), 0)
     col_id = lax.broadcasted_iota(jnp.int32, (32, 2048), 1)
     wanted = lax.rem(row_id, 16) * 128 + jnp.where(row_id < 16, 0, 127)
@@ -256,7 +256,7 @@
             target[d, h, 32:48, :] = pltpu.roll(row, 127, 1)
             return 0
 
-        lax.fori_loop(0, 128, spread, 0, unroll=8)
+        lax.fori_loop(0, 128, spread, 0, unroll=16)
 
     def close_own(edge, target):
         left_edge = only(inside_left, edge[0, 1, 1])
@@ -270,7 +270,7 @@
             target[d, h, 32:48, :] = jnp.where(lane == 127, right, target[d, h, 32:48, :])
             return 0
 
-        lax.fori_loop(0, 128, close, 0, unroll=8)
+        lax.fori_loop(0, 128, close, 0, unroll=16)
 
     shift_own(vol, stack0)
     wait_recv(near_in)
@@ -292,7 +292,7 @@
         top0[lax.div(d, 2), pl.ds(lax.div(h, 2), 2)] = top
         return 0
 
-    lax.fori_loop(0, 16, encode, 0, unroll=4)
+    lax.fori_loop(0, 16, encode, 0, unroll=8)
     for d in range(4):
         both = jnp.dot(top0[d].reshape(128, 128), pick[...], preferred_element_type=F32)
         best = jnp.maximum(both[:, :128], both[:, 128:])
@@ -513,7 +513,7 @@
             part1[i, j] = combine(total, 64, 1, j) + off1[...]
         return 0
 
-    lax.fori_loop(0, 15, upper_one_skip, 0, unroll=3)
+    lax.fori_loop(0, 15, upper_one_skip, 0, unroll=5)
 
     wait_recv(rowsz + edgesz)
     close_own(edgez, stack0)
@@ -528,7 +528,7 @@
             part0[d + j, pl.ds(h, 4)] = value.reshape(4, 16, 128)
         return 0
 
-    lax.fori_loop(0, 16, decode_skip, 0, unroll=4)
+    lax.fori_loop(0, 16, decode_skip, 0, unroll=8)
 
     wait_recv(edges2 + pools2)
     for side in range(2):
@@ -628,7 +628,7 @@
             low2[d + j, h] = jnp.where(keeps(d + j - 1, h - 1, 2, 4), value, 0.0).astype(BF16)
         return 0
 
-    lax.fori_loop(0, 12, upper_two, 0, unroll=3)
+    lax.fori_loop(0, 12, upper_two, 0, unroll=6)
     for d in range(4):
         for h, row in enumerate(lifts(lift1, [low2[d, h] for h in range(6)])):
             lifted1[d, h] = row
@@ -688,7 +688,7 @@
             out_ref[c, pl.ds(d, 2)] = rows.reshape(2, 16, 128)
         return 0
 
-    lax.fori_loop(0, 4, decode, 0)
+    lax.fori_loop(0, 4, decode, 0, unroll=2)
 
     wait_send(sent)
 

time: 54.5 us -> 52.7 us (0.967)
  Pallas kernels: 53.6 us -> 51.8 us
    pallas_call x1, Pallas kernels: 53.6 us -> 51.8 us  [per_device(): pl.pallas_call(kernel, out_shape=pltpu.VMEM(volume.shape, BF16), in_specs...]
where the time goes in v5:
time: 52.7 us; the launch traced here: 52.6 us
  Pallas kernels  51.8 us (98%)
  local copies, waits for them, and re-layouts  0.8 us (2%)
    pallas_call x1, Pallas kernels, per_device(): pl.pallas_call(kernel, out_shape=pltpu.VMEM(volume.shape, BF16), in_specs...  51.8 us

profile of v5, /device:TPU:1, one launch (start us, length us, event | category | flops | bytes accessed | tf_op | source)
XLA Modules:
  0.0 52.6 jit_solution(4737615707095440850)
XLA Ops:
  0.0 51.8 %shard_map.172 = bf16[16,8,16,128]{3,2,1,0:T(8,128)(2,1)S(1)} custom-call(bf16[16,8,16,128]{3,2,1,0:T(8,128)(2,1)} %refs_0_.1, bf16[27,16,16]{2,1,0:T(8,128)(2,1)} %bitcast.32, f32[1,16]{1,0:T(1,128)} %bitcast.35, bf16[27,16,32]{2,1,0:T(8,128)(2,1)} %bitcast.33, f32[1,32]{1,0:T(1,128)} %bitcast.36, bf16[27,32,64]{2,1,0:T(8,128)(2,1)} %bitcast.30, ...), custom_call_target="tpu_custom_call" | custom-call | tf_op jit(solution)/shard_map/pallas_call | solution.py:762
  51.9 0.8 %copy.20 = bf16[16,8,16,128]{3,2,1,0:T(8,128)(2,1)} copy(bf16[16,8,16,128]{3,2,1,0:T(8,128)(2,1)S(1)} %shard_map.172) | data formatting | bytes 1048576

commit v6 on v5

--- a/solution.py
+++ b/solution.py
@@ -730,7 +730,7 @@
         return pltpu.VMEM((rows, 128), F32)
 
     scratch = [
-        wide(2048), tile(10, 18, 16, 128), tile(2, 3, 3, 16, 128), tile(2, 16, 128), tile(10, 18, 48, 128),
+        wide(2176), tile(10, 18, 16, 128), tile(2, 3, 3, 16, 128), tile(2, 16, 128), tile(10, 18, 48, 128),
         tile(10, 18, 16, 128), tile(2, 3, 3, 16, 128), tile(2, 16, 128),
         tile(4, 8, 16, 128), tile(10, 14, 16, 128), tile(10, 8, 16, 128), tile(2, 3, 3, 16, 128), tile(2, 16, 128),
         tile(8, 12, 32, 128), tile(4, 6, 64, 128), tile(4, 6, 32, 128), tile(4, 6, 32, 128),

time: 52.7 us -> 52.7 us (level)
  no operation moved by 1% of the time
where the time goes in v6:
time: 52.7 us; the launch traced here: 52.6 us
  Pallas kernels  51.8 us (98%)
  local copies, waits for them, and re-layouts  0.8 us (2%)
    pallas_call x1, Pallas kernels, per_device(): pl.pallas_call(kernel, out_shape=pltpu.VMEM(volume.shape, BF16), in_specs...  51.8 us

profile of v6, /device:TPU:1, one launch (start us, length us, event | category | flops | bytes accessed | tf_op | source)
XLA Modules:
  0.0 52.6 jit_solution(16728385193934544054)
XLA Ops:
  0.0 51.8 %shard_map.172 = bf16[16,8,16,128]{3,2,1,0:T(8,128)(2,1)S(1)} custom-call(bf16[16,8,16,128]{3,2,1,0:T(8,128)(2,1)} %refs_0_.1, bf16[27,16,16]{2,1,0:T(8,128)(2,1)} %bitcast.32, f32[1,16]{1,0:T(1,128)} %bitcast.35, bf16[27,16,32]{2,1,0:T(8,128)(2,1)} %bitcast.33, f32[1,32]{1,0:T(1,128)} %bitcast.36, bf16[27,32,64]{2,1,0:T(8,128)(2,1)} %bitcast.30, ...), custom_call_target="tpu_custom_call" | custom-call | tf_op jit(solution)/shard_map/pallas_call | solution.py:762
  51.9 0.8 %copy.20 = bf16[16,8,16,128]{3,2,1,0:T(8,128)(2,1)} copy(bf16[16,8,16,128]{3,2,1,0:T(8,128)(2,1)S(1)} %shard_map.172) | data formatting | bytes 1048576
